TPU v7x, 128 devices: a whole 4x4x4 slice. The times are simulated.
128 devices in a mesh: row: 8 (over z_hi, x), col: 16 (over z_lo, y, core).
Axes of the slice: x: 4, y: 4, z: 4 (z_hi: 2, z_lo: 2; z = z_hi * 2 + z_lo), core: 2. Of those that a mesh axis runs over, the one named last changes fastest.
Arguments:
- pair_state: bfloat16 [512, 512, 128], P('row', 'col'), may hold values from -6 to 6
- proj_weight: bfloat16 [2, 128, 640], replicated, may hold values from -0.5 to 0.5
- out_weight: bfloat16 [2, 128, 128], replicated, may hold values from -0.5 to 0.5
Outputs:
- pair_out: bfloat16 [512, 512, 128], P('row', 'col')
All inputs are finite; a program needn't handle non-finite values.
Results may differ from a plain program's by a relative error of at most 0.015.
Values may be sent and summed in bfloat16 or wider, within the bound.
A program may use at most 128 MiB of HBM per device.

v0:
```python
import jax
import jax.numpy as jnp
from jax import lax
from jax.sharding import PartitionSpec as P


def spread_2(value, axis, source):
    kept = jnp.where(lax.axis_index(axis) == source, value, 0).astype(value.dtype)
    return lax.psum(kept, axis)


def normalize(values):
    center = values - jnp.mean(values, axis=-1, keepdims=True)
    spread = jnp.mean(center * center, axis=-1, keepdims=True)
    return center * lax.rsqrt(spread + 1e-05)


def project(pair, weight, hidden):
    row_count, col_count, width = pair.shape
    normed = (
        normalize(pair.astype(jnp.float32))
        .astype(jnp.bfloat16)
        .reshape(row_count * col_count, width)
    )
    projected = jnp.dot(normed, weight, preferred_element_type=jnp.float32)
    left_proj = (jax.nn.sigmoid(projected[:, :hidden]) * projected[:, hidden : 2 * hidden]).astype(
        jnp.bfloat16
    )
    right_proj = (
        jax.nn.sigmoid(projected[:, 2 * hidden : 3 * hidden])
        * projected[:, 3 * hidden : 4 * hidden]
    ).astype(jnp.bfloat16)
    gating = jax.nn.sigmoid(projected[:, 4 * hidden :])
    return (
        left_proj.reshape(row_count, col_count, hidden),
        right_proj.reshape(row_count, col_count, hidden),
        gating,
    )


def finish(pair, gating, mixed_sum, out_proj):
    row_count, col_count, width = pair.shape
    mixnorm = normalize(mixed_sum).astype(jnp.bfloat16).reshape(row_count * col_count, -1)
    output = jnp.dot(mixnorm, out_proj, preferred_element_type=jnp.float32)
    updated = pair.astype(jnp.float32).reshape(row_count * col_count, width) + gating * output
    return updated.astype(jnp.bfloat16).reshape(row_count, col_count, width)


def shards(pair_state, proj_weight, out_weight):
    row_count, col_count, width = pair_state.shape
    fold_ratio = row_count // col_count
    hidden = out_weight.shape[1]
    left_proj, right_proj, gating = project(pair_state, proj_weight[0], hidden)
    left_rows = lax.all_gather(left_proj, "col", axis=1, tiled=True)
    right_rows = lax.all_gather(right_proj, "col", axis=1, tiled=True)
    column = lax.axis_index("col")
    segment = lax.dynamic_slice_in_dim(right_rows, column % fold_ratio * col_count, col_count, 0)
    right_mine = spread_2(segment, "row", column // fold_ratio)
    mixed_sum = jnp.einsum(
        "ikc,jkc->ijc", left_rows, right_mine, preferred_element_type=jnp.float32
    )
    first_pair = finish(pair_state, gating, mixed_sum, out_weight[0])
    left_proj, right_proj, gating = project(first_pair, proj_weight[1], hidden)
    left_cols = lax.all_gather(left_proj, "row", axis=0, tiled=True)
    root_base = lax.axis_index("row") * fold_ratio
    blocks = []
    for member in range(fold_ratio):
        blocks.append(spread_2(left_cols, "col", root_base + member))
    left_mine = jnp.concatenate(blocks, axis=1)
    right_cols = lax.all_gather(right_proj, "row", axis=0, tiled=True)
    mixed_sum = jnp.einsum(
        "kic,kjc->ijc", left_mine, right_cols, preferred_element_type=jnp.float32
    )
    return finish(first_pair, gating, mixed_sum, out_weight[1])


def solution(mesh):
    in_specs = (P("row", "col", None), P(), P())
    out_specs = P("row", "col", None)
    return jax.shard_map(shards, mesh=mesh, in_specs=in_specs, out_specs=out_specs, check_vma=False)
```

profile of v0, /device:TPU:0, one launch (start us, length us, event | category | flops | bytes accessed | tf_op | source)
XLA Modules:
  0.0 602.1 jit_solution(13909480360892368294)
XLA Ops:
  6.5 1.4 convert_reduce_fusion
  7.9 0.1 copy.46
  8.0 0.1 copy.47
  8.1 1.7 multiply_reduce_fusion.3
  9.8 0.1 copy.48
  9.9 0.1 copy.49
  9.9 1.7 multiply_convert_fusion.3
  11.6 1.7 fusion.35
  13.4 2.4 copy-done
  15.7 0.6 fusion.20
  16.3 1.0 copy.50
  17.3 0.0 all-gather.5.cloned.1.call-update
  17.3 0.0 all-gather.7.cloned.1.call-start
  17.3 2.6 copy.52
  20.0 0.0 all-gather.7.cloned.1.call-update
  20.0 0.0 all-reduce.4.cloned.1.call-start
  20.1 52.0 %all-gather.5.cloned.1.call-done = bf16[64,512,128]{2,0,1:T(8,128)(2,1)} async-done(((bf16[64,32,128]{2,0,1:T(8,128)(2,1)}), bf16[64,512,128]{2,0,1:T(8,128)(2,1)}) %all-gather.5.cloned.1.call-update) | async-done | bytes 8388624 | tf_op jit(solution)/shard_map/all_gather | solution.py:55
  72.1 4.9 constant_dynamic-slice_fusion
  77.0 8.8 %copy.58 = bf16[32,512,128]{1,0,2:T(8,128)(2,1)} copy(bf16[32,512,128]{2,0,1:T(8,128)(2,1)} %constant_dynamic-slice_fusion) | data formatting | bytes 8388608
  85.7 4.4 broadcast_select_fusion.2
  90.2 0.0 all-reduce.4.cloned.1.call-update
  90.2 0.2 all-gather.11.cloned.1.call-start
  90.4 75.8 %all-gather.7.cloned.1.call-done = bf16[64,512,128]{0,1,2:T(8,128)(2,1)} async-done(((bf16[64,32,128]{0,1,2:T(8,128)(2,1)}), bf16[64,512,128]{0,1,2:T(8,128)(2,1)}) %all-gather.7.cloned.1.call-update) | async-done | bytes 8388624 | tf_op jit(solution)/shard_map/all_gather | solution.py:54
  166.2 113.1 %all-reduce.4.cloned.1.call-done = bf16[32,512,128]{1,0,2:T(8,128)(2,1)} async-done(((bf16[32,512,128]{1,0,2:T(8,128)(2,1)}), bf16[32,512,128]{1,0,2:T(8,128)(2,1)}) %all-reduce.4.cloned.1.call-update) | async-done | bytes 4194320 | tf_op jit(solution)/shard_map/psum | solution.py:9
  279.3 9.7 %bitcast_reduce_fusion.1 = (f32[64,32]{0,1:T(8,128)S(1)}, f32[128,32,64]{2,1,0:T(8,128)S(1)}) fusion(bf16[32,512,128]{1,0,2:T(8,128)(2,1)} %all-reduce.4.cloned.1.call-done, bf16[64,512,128]{0,1,2:T(8,128)(2,1)} %all-gather.7.cloned.1.call-done), kind=kOutput, calls=%fused_computation.17 | convolution fusion | flops 268695552 | bytes 13639680 | tf_op jit(solution)/shard_map/ikc,jkc->ijc/dot_general | solution.py:59
  289.0 0.3 multiply_reduce_fusion.1
  289.4 0.3 multiply_convert_fusion.1
  289.6 1.5 copy.53
  291.2 1.8 fusion.44
  293.0 0.6 multiply_reduce_fusion.2
  293.6 1.0 fusion.31
  294.7 2.3 copy-done.1
  297.0 1.5 fusion.9
  298.6 0.0 all-gather.9.cloned.1.call-start
  298.6 0.5 all-gather.9.cloned.1.call-update
  299.1 0.3 all-reduce.6.cloned.1.call-start
  299.4 69.4 %all-gather.11.cloned.1.call-done = bf16[512,32,128]{2,1,0:T(8,128)(2,1)} async-done(((bf16[64,32,128]{2,1,0:T(8,128)(2,1)}), bf16[512,32,128]{2,1,0:T(8,128)(2,1)}) %all-gather.11.cloned.1.call-update) | async-done | bytes 4194320 | tf_op jit(solution)/shard_map/all_gather | solution.py:64
  368.8 8.6 %copy.54 = bf16[512,32,128]{0,1,2:T(8,128)(2,1)} copy(bf16[512,32,128]{2,1,0:T(8,128)(2,1)} %all-gather.11.cloned.1.call-done) | data formatting | bytes 8388608 | tf_op jit(solution)/shard_map/all_gather | solution.py:64
  377.4 6.3 %broadcast_select_fusion.1 = (bf16[512,32,128]{0,1,2:T(8,128)(2,1)}, bf16[512,32,128]{0,1,2:T(8,128)(2,1)}) fusion(bf16[512,32,128]{0,1,2:T(8,128)(2,1)} %copy.54, pred[]{:T(512)S(6)} %eq.12, pred[]{:T(512)S(6)} %eq.13), kind=kLoop, calls=%fused_computation.5 | loop fusion | flops 4194304 | bytes 12582914 | tf_op jit(solution)/shard_map/jit(_where)/select_n | solution.py:8
  383.6 0.0 all-reduce.6.cloned.1.call-update
  383.7 56.7 %all-gather.9.cloned.1.call-done = bf16[512,32,128]{2,1,0:T(8,128)(2,1)} async-done(((bf16[64,32,128]{2,1,0:T(8,128)(2,1)}), bf16[512,32,128]{2,1,0:T(8,128)(2,1)}) %all-gather.9.cloned.1.call-update) | async-done | bytes 4194320 | tf_op jit(solution)/shard_map/all_gather | solution.py:70
  440.3 8.6 %copy.56 = bf16[512,32,128]{0,1,2:T(8,128)(2,1)} copy(bf16[512,32,128]{2,1,0:T(8,128)(2,1)} %all-gather.9.cloned.1.call-done) | data formatting | bytes 8388608 | tf_op jit(solution)/shard_map/all_gather | solution.py:70
  448.9 134.8 %all-reduce.6.cloned.1.call-done = (bf16[512,32,128]{0,1,2:T(8,128)(2,1)}, bf16[512,32,128]{0,1,2:T(8,128)(2,1)}) async-done(((bf16[512,32,128]{0,1,2:T(8,128)(2,1)}, bf16[512,32,128]{0,1,2:T(8,128)(2,1)}), (bf16[512,32,128]{0,1,2:T(8,128)(2,1)}, bf16[512,32,128]{0,1,2:T(8,128)(2,1)})) %all-reduce.6.cloned.1.call-update) | async-done | bytes 8388624 | tf_op jit(solution)/shard_map/psum | solution.py:9
  583.7 7.0 %bitcast_reduce_fusion = (f32[64,32]{0,1:T(8,128)S(1)}, f32[128,32,64]{2,1,0:T(8,128)S(1)}) fusion(bf16[512,32,128]{0,1,2:T(8,128)(2,1)} %copy.56, bf16[512,32,128]{0,1,2:T(8,128)(2,1)} %get-tuple-element.5, bf16[512,32,128]{0,1,2:T(8,128)(2,1)} %get-tuple-element.6), kind=kOutput, calls=%fused_computation.15 | convolution fusion | flops 285472768 | bytes 13639680 | tf_op jit(solution)/shard_map/kic,kjc->ijc/dot_general | solution.py:71
  590.7 0.3 multiply_reduce_fusion
  591.0 0.3 multiply_convert_fusion
  591.3 1.5 copy.57
  592.8 2.4 fusion.8
  (18 shorter events, 0.1 us)
Async XLA Ops:
  6.5 65.5 %all-gather.5.cloned.1.call-start = ((), (), s32[]{:S(2)}) async-start(), calls=%async_computation | async-start | bytes 8912896 | tf_op jit(solution)/shard_map/all_gather | solution.py:55
  13.3 2.4 copy-start
  17.3 148.9 %all-gather.7.cloned.1.call-start = ((), (), s32[]{:S(2)}) async-start(), calls=%async_computation.2 | async-start | bytes 17825792 | tf_op jit(solution)/shard_map/all_gather | solution.py:54
  20.0 259.3 %all-reduce.4.cloned.1.call-start = ((), (), s32[]{:S(2)}) async-start(), calls=%async_computation.1 | async-start | bytes 8388608 | tf_op jit(solution)/shard_map/psum | solution.py:9
  90.2 278.6 %all-gather.11.cloned.1.call-start = ((), (), s32[]{:S(2)}) async-start(), calls=%async_computation.4 | async-start | bytes 4718592 | tf_op jit(solution)/shard_map/all_gather | solution.py:64
  289.0 2.2 copy-start.2
  289.0 2.2 copy-start.4
  289.6 4.0 copy-start.3
  294.7 2.3 copy-start.1
  298.6 141.8 %all-gather.9.cloned.1.call-start = ((), (), s32[]{:S(2)}) async-start(), calls=%async_computation.3 | async-start | bytes 4718592 | tf_op jit(solution)/shard_map/all_gather | solution.py:70
  299.1 284.5 %all-reduce.6.cloned.1.call-start = ((), (), s32[]{:S(2)}) async-start(), calls=%async_computation.5 | async-start | bytes 16777216 | tf_op jit(solution)/shard_map/psum | solution.py:9
Sparse Core Ops, SparseCore 0:
  17.4 54.6 all-gather.4
  73.7 92.4 all-gather.6
  168.8 110.5 all-reduce.3
  298.7 70.0 all-gather.10
  371.0 69.2 all-gather.8
  442.7 140.9 all-reduce.5
where the time goes:
time: 603 us; the launch traced here: 602 us
  waiting for transfers between devices  502 us (83%)
  local copies, waits for them, and re-layouts  42.5 us (7%)
  matrix products  23.6 us (4%)
  other arithmetic  19.4 us (3%)
  between operations  13.7 us (2%)
    psum x2, waiting for transfers between devices, spread_2(): return lax.psum(kept, axis)  248 us
    all_gather x1, waiting for transfers between devices, shards(): left_rows = lax.all_gather(left_proj, 'col', axis=1, tiled=True)  75.8 us
    all_gather x1, waiting for transfers between devices, shards(): left_cols = lax.all_gather(left_proj, 'row', axis=0, tiled=True)  69.4 us
    all_gather x1, waiting for transfers between devices, shards(): right_cols = lax.all_gather(right_proj, 'row', axis=0, tiled=True)  56.7 us
    all_gather x1, waiting for transfers between devices, shards(): right_rows = lax.all_gather(right_proj, 'col', axis=1, tiled=True)  52 us
    unnamed x11, local copies, waits for them, and re-layouts  13.5 us
  transfers between devices with their start and end apart: 6, of which 6 were waited for; matrix products, arithmetic and copies ran while one was open for 7% of the time, Pallas kernels for 0%

commit v1 on v0

v1 whole, which is shorter than its diff:
```python
import functools

import jax
import jax.numpy as jnp
from jax import lax
from jax.experimental import pallas as pl
from jax.experimental.pallas import tpu as pltpu
from jax.sharding import PartitionSpec as P

F32 = jnp.float32
BF16 = jnp.bfloat16
MESH = pl.DeviceIdType.MESH


def sigmoid(x):
    return 0.5 * jnp.tanh(0.5 * x) + 0.5


def normalize(x):
    center = x - jnp.mean(x, axis=0, keepdims=True)
    spread = jnp.mean(center * center, axis=0, keepdims=True)
    return center * lax.rsqrt(spread + 1e-05)


def interleave(even, odd):
    first = jnp.concatenate([even[..., :64], odd[..., :64]], axis=-1)
    second = jnp.concatenate([even[..., 64:], odd[..., 64:]], axis=-1)
    return first, second


def kernel(
    pair_ref,
    proj_ref,
    out_proj_ref,
    out_ref,
    proj_t,
    out_proj_t,
    state,
    normed,
    gating,
    staged,
    mixnorm,
    final,
    left_op0,
    left_op1,
    partial,
    send_left,
    send_right,
    recv_left,
    recv_right,
    sibling_left,
    half_send,
    half_recv,
    send_mixed,
    recv_mixed,
    left_send_sem,
    left_recv_sem,
    right_send_sem,
    right_recv_sem,
    sib_send_sem,
    sib_recv_sem,
    half_send_sem,
    half_recv_sem,
    mixed_send_sem,
    mixed_recv_sem,
):
    r = lax.axis_index("row")
    col = lax.axis_index("col")
    q = col // 2
    core = col % 2
    chip = r * 8 + q

    def device(dest_r, dest_q):
        return (dest_r, dest_q * 2 + core)

    sibling = (r, q * 2 + 1 - core)

    barrier = pltpu.get_barrier_semaphore()

    def greet(d, carry):
        other = lax.rem(chip + d, 64)
        pl.semaphore_signal(barrier, inc=1, device_id=device(other // 8, other % 8), device_id_type=MESH)
        return carry

    lax.fori_loop(1, 64, greet, 0)
    pl.semaphore_signal(barrier, inc=1, device_id=sibling, device_id_type=MESH)

    for u in range(2):
        proj_t[u] = proj_ref[u].T
        out_proj_t[u] = out_proj_ref[u].T

    pair = jnp.swapaxes(pair_ref[...], 0, 1)
    final[...] = pair.reshape(2, 16, 64, 128)

    def load(t, carry):
        for h in range(2):
            block = final[:, 2 * t + h].reshape(128, 128).astype(F32).T
            state[t, :, 128 * h : 128 * h + 128] = block
        normed[t] = normalize(state[t]).astype(BF16)
        return carry

    lax.fori_loop(0, 8, load, 0)

    def gated(u, first, dest):
        def step(t, carry):
            p = jnp.dot(proj_t[u, first : first + 256], normed[t], preferred_element_type=F32)
            value = (sigmoid(p[:128]) * p[128:]).astype(BF16)
            for h in range(2):
                staged[2 * t + h] = value[:, 128 * h : 128 * h + 128]
            return carry

        lax.fori_loop(0, 8, step, 0)
        dest[u] = jnp.swapaxes(staged[...], 0, 1).reshape(64, 2, 16, 128)

    def gate(u):
        def step(t, carry):
            p = jnp.dot(proj_t[u, 512:640], normed[t], preferred_element_type=F32)
            gating[t] = sigmoid(p)
            return carry

        lax.fori_loop(0, 8, step, 0)

    def push(src, dst, send_sem, recv_sem, dest_r, dest_q):
        own = jnp.logical_and(dest_r == r, dest_q == q)

        @pl.when(own)
        def _():
            pltpu.make_async_copy(src, dst, recv_sem).start()

        @pl.when(jnp.logical_not(own))
        def _():
            pltpu.make_async_remote_copy(
                src_ref=src,
                dst_ref=dst,
                send_sem=send_sem,
                recv_sem=recv_sem,
                device_id=device(dest_r, dest_q),
                device_id_type=MESH,
            ).start()

    def send_all_left(u):
        slot = recv_left.at[0, r, q] if u == 0 else recv_left.at[1, q, r]

        def step(d, carry):
            other = lax.rem(chip + 37 * d, 64)
            push(send_left.at[u, other], slot, left_send_sem.at[u], left_recv_sem.at[u], other // 8, other % 8)
            return carry

        lax.fori_loop(0, 64, step, 0)

    def send_all_right(u):
        slot = recv_right.at[0, r, q] if u == 0 else recv_right.at[1, q, r]
        mine = r // 2 if u == 0 else q // 2

        def step(d, carry):
            group = lax.rem(mine + 4 - d // 16, 4)
            one, eight = (d // 8) % 2, d % 8
            if u == 0:
                dest_r, dest_q = group * 2 + (one + r) % 2, (eight + q) % 8
            else:
                dest_r, dest_q = (eight + r) % 8, group * 2 + (one + q) % 2
            push(
                send_right.at[u, dest_r * 8 + dest_q],
                slot,
                right_send_sem.at[u],
                right_recv_sem.at[u, mine],
                dest_r,
                dest_q,
            )
            return carry

        lax.fori_loop(0, 64, step, 0)

    def give_back(u, group, c, value):
        for qq in range(2):
            for m in range(4):
                lower = value[qq, :16, 128 * m : 128 * m + 128]
                upper = value[qq, 16:, 128 * m : 128 * m + 128]
                first, second = interleave(lower, upper)
                send_mixed[u, 2 * group + qq, 2 * m, c] = first
                send_mixed[u, 2 * group + qq, 2 * m + 1, c] = second

    def send_back(u, group):
        def step(d, carry):
            dest_q, dest_r = 2 * group + d // 8, (r + d) % 8
            push(
                send_mixed.at[u, dest_q, dest_r],
                recv_mixed.at[u, chip],
                mixed_send_sem.at[u],
                mixed_recv_sem.at[u],
                dest_r,
                dest_q,
            )
            return carry

        lax.fori_loop(0, 16, step, 0)

    def wait_all(ref, sem):
        pltpu.make_async_copy(ref, ref, sem).wait()

    def outgoing():
        wait_all(recv_left.at[0], left_recv_sem.at[0])
        for c in range(2):
            for m in range(4):
                first, second = interleave(recv_left[0, 2 * m, :, c], recv_left[0, 2 * m + 1, :, c])
                left_op0[c, 0, :, :, 128 * m : 128 * m + 128] = first
                left_op0[c, 1, :, :, 128 * m : 128 * m + 128] = second

        def half_copy(t):
            return pltpu.make_async_remote_copy(
                src_ref=half_send.at[t],
                dst_ref=half_recv.at[t],
                send_sem=half_send_sem.at[t],
                recv_sem=half_recv_sem.at[t],
                device_id=sibling,
                device_id_type=MESH,
            )

        def finish_group(t):
            group = lax.rem(r // 2 + t, 4)
            half_copy(t).wait_recv()
            for c in range(2):
                total = partial[t % 2, c, :, core] + half_recv[t, c].astype(F32)
                give_back(0, group, c, total.astype(BF16))
            send_back(0, group)

        for t in range(4):
            group = lax.rem(r // 2 + t, 4)
            wait_all(recv_right.at[0, pl.ds(2 * group, 2)], right_recv_sem.at[0, group])
            for c in range(2):
                first, second = interleave(recv_right[0, 2 * group, :, c], recv_right[0, 2 * group + 1, :, c])
                right = jnp.concatenate([first.reshape(128, 128), second.reshape(128, 128)], axis=0)
                product = lax.dot_general(
                    right, left_op0[c].reshape(256, 512), (((0,), (0,)), ((), ())), preferred_element_type=F32
                )
                partial[t % 2, c] = product.reshape(2, 2, 32, 512)
                half_send[t, c] = partial[t % 2, c, :, 1 - core].astype(BF16)
            half_copy(t).start()
            if t:
                finish_group(t - 1)
        finish_group(3)
        for t in range(4):
            half_copy(t).wait_send()

    def incoming():
        wait_all(recv_left.at[1], left_recv_sem.at[1])
        swap = pltpu.make_async_remote_copy(
            src_ref=recv_left.at[1],
            dst_ref=sibling_left,
            send_sem=sib_send_sem,
            recv_sem=sib_recv_sem,
            device_id=sibling,
            device_id_type=MESH,
        )
        swap.start()

        def arrange(blocks, which):
            for c in range(2):
                for m in range(4):
                    first, second = interleave(blocks[:, 2 * m, c], blocks[:, 2 * m + 1, c])
                    left_op1[c, :, which, 0, :, 128 * m : 128 * m + 128] = first
                    left_op1[c, :, which, 1, :, 128 * m : 128 * m + 128] = second

        arrange(recv_left.at[1], core)
        swap.wait_recv()
        arrange(sibling_left, 1 - core)

        for t in range(4):
            group = lax.rem(q // 2 + t, 4)
            wait_all(recv_right.at[1, pl.ds(2 * group, 2)], right_recv_sem.at[1, group])
            for c in range(2):
                columns = []
                for m in range(4):
                    even = recv_right[1, pl.ds(2 * group, 2), 2 * m, c]
                    odd = recv_right[1, pl.ds(2 * group, 2), 2 * m + 1, c]
                    columns.append(jnp.stack(interleave(even, odd), axis=1).reshape(64, 128))
                right = jnp.concatenate(columns, axis=1)
                product = lax.dot_general(
                    right, left_op1[c].reshape(512, 512), (((1,), (1,)), ((), ())), preferred_element_type=F32
                )
                give_back(1, group, c, product.astype(BF16).reshape(2, 32, 512))
            send_back(1, group)
        swap.wait_send()

    def absorb(u):
        wait_all(recv_mixed.at[u], mixed_recv_sem.at[u])
        mixed = recv_mixed[u].reshape(128, 16, 128).astype(F32)
        norm = jnp.swapaxes(normalize(mixed).astype(BF16), 0, 1)
        for t in range(8):
            for h in range(2):
                mixnorm[t, :, 128 * h : 128 * h + 128] = norm[2 * t + h]

        def step(t, carry):
            output = jnp.dot(out_proj_t[u], mixnorm[t], preferred_element_type=F32)
            updated = state[t] + gating[t] * output
            if u == 0:
                updated = updated.astype(BF16).astype(F32)
                state[t] = updated
                normed[t] = normalize(updated).astype(BF16)
            else:
                for h in range(2):
                    block = updated[:, 128 * h : 128 * h + 128].T.astype(BF16)
                    final[:, 2 * t + h] = block.reshape(2, 64, 128)
            return carry

        lax.fori_loop(0, 8, step, 0)

    gated(0, 0, send_left)
    pl.semaphore_wait(barrier, 64)
    send_all_left(0)
    gated(0, 256, send_right)
    send_all_right(0)
    gate(0)
    outgoing()
    absorb(0)
    gated(1, 0, send_left)
    send_all_left(1)
    gated(1, 256, send_right)
    send_all_right(1)
    gate(1)
    incoming()
    absorb(1)
    out_ref[...] = final[...].reshape(32, 64, 128)

    for u in range(2):
        sent = pl.ds(0, 63)
        wait_all(send_left.at[u, sent], left_send_sem.at[u])
        wait_all(send_right.at[u, sent], right_send_sem.at[u])
        wait_all(recv_mixed.at[u, sent], mixed_send_sem.at[u])


def shards(pair_state, proj_weight, out_weight):
    vmem = pl.BlockSpec(memory_space=pltpu.VMEM)
    dma = pltpu.SemaphoreType.DMA
    out = pl.pallas_call(
        kernel,
        out_shape=jax.ShapeDtypeStruct((32, 64, 128), BF16),
        in_specs=[vmem] * 3,
        out_specs=vmem,
        scratch_shapes=[
            pltpu.VMEM((2, 640, 128), BF16),
            pltpu.VMEM((2, 128, 128), BF16),
            pltpu.VMEM((8, 128, 256), F32),
            pltpu.VMEM((8, 128, 256), BF16),
            pltpu.VMEM((8, 128, 256), F32),
            pltpu.VMEM((16, 128, 128), BF16),
            pltpu.VMEM((8, 128, 256), BF16),
            pltpu.VMEM((2, 16, 64, 128), BF16),
            pltpu.VMEM((2, 2, 8, 16, 512), BF16),
            pltpu.VMEM((2, 8, 2, 2, 16, 512), BF16),
            pltpu.VMEM((2, 2, 2, 2, 32, 512), F32),
            pltpu.VMEM((2, 64, 2, 16, 128), BF16),
            pltpu.VMEM((2, 64, 2, 16, 128), BF16),
            pltpu.VMEM((2, 8, 8, 2, 16, 128), BF16),
            pltpu.VMEM((2, 8, 8, 2, 16, 128), BF16),
            pltpu.VMEM((8, 8, 2, 16, 128), BF16),
            pltpu.VMEM((4, 2, 2, 32, 512), BF16),
            pltpu.VMEM((4, 2, 2, 32, 512), BF16),
            pltpu.VMEM((2, 8, 8, 2, 16, 128), BF16),
            pltpu.VMEM((2, 64, 2, 16, 128), BF16),
            dma((2,)),
            dma((2,)),
            dma((2,)),
            dma((2, 4)),
            dma,
            dma,
            dma((4,)),
            dma((4,)),
            dma((2,)),
            dma((2,)),
        ],
        compiler_params=pltpu.CompilerParams(
            collective_id=0, has_side_effects=True, vmem_limit_bytes=48 * 2**20
        ),
    )(pair_state, proj_weight, out_weight)
    return jnp.transpose(out, (1, 0, 2))


def solution(mesh):
    in_specs = (P("row", "col", None), P(), P())
    out_specs = P("row", "col", None)
    return jax.shard_map(shards, mesh=mesh, in_specs=in_specs, out_specs=out_specs, check_vma=False)
```

time: 603 us -> 71.3 us (0.12)
  waiting for transfers between devices: 502 us -> 0 us
  Pallas kernels: 0 us -> 66.2 us
  local copies, waits for them, and re-layouts: 42.5 us -> 3.99 us
  matrix products: 23.6 us -> 0 us
  other arithmetic: 19.4 us -> 0 us
  between operations: 13.7 us -> 0.01 us
    all_gather x4 -> x0, waiting for transfers between devices: 254 us -> none  [the longest x1 75.8 us: shards(): left_rows = lax.all_gather(left_proj, 'col', axis=1, tiled=True)]
    psum x2 -> x0, waiting for transfers between devices: 248 us -> none  [spread_2(): return lax.psum(kept, axis)]
    pallas_call x0 -> x1, Pallas kernels: none -> 66.2 us  [shards(): pl.pallas_call(kernel, out_shape=jax.ShapeDtypeStruct((32, 64, 128), BF16...]
    dot_general x6 -> x0, matrix products: 23.6 us -> none  [the longest x1 9.67 us: shards(): jnp.einsum('ikc,jkc->ijc', left_rows, right_mine, preferred_element_type=...]
    all_gather x2 -> x0, local copies, waits for them, and re-layouts: 17.2 us -> none  [the longest x1 8.62 us: shards(): right_cols = lax.all_gather(right_proj, 'row', axis=0, tiled=True)]
    select_n x2 -> x0, other arithmetic: 10.7 us -> none  [spread_2(): jnp.where(lax.axis_index(axis) == source, value, 0).astype(value.dtype)]
    unnamed x11 -> x6, local copies, waits for them, and re-layouts: 13.5 us -> 2.85 us
  transfers between devices with their start and end apart: 6 -> 0, of which waited for: 6 -> 0; matrix products, arithmetic and copies ran while one was open for 7% -> 0% of each run, Pallas kernels for 0% -> 0%
where the time goes in v1:
time: 71.3 us; the launch traced here: 70.2 us
  Pallas kernels  66.2 us (93%)
  local copies, waits for them, and re-layouts  3.99 us (6%)
    pallas_call x1, Pallas kernels, shards(): pl.pallas_call(kernel, out_shape=jax.ShapeDtypeStruct((32, 64, 128), BF16...  66.2 us
    unnamed x6, local copies, waits for them, and re-layouts  2.85 us

profile of v1, /device:TPU:0, one launch (start us, length us, event | category | flops | bytes accessed | tf_op | source)
XLA Modules:
  0.0 70.2 jit_solution(15053661679043267315)
XLA Ops:
  0.0 0.0 copy-start
  0.0 1.0 %copy-done = bf16[64,32,128]{2,1,0:T(8,128)(2,1)S(1)} copy-done((bf16[64,32,128]{2,1,0:T(8,128)(2,1)S(1)}, bf16[64,32,128]{2,1,0:T(8,128)(2,1)}, u32[]{:S(2)}) %copy-start) | copy-done | bytes 524312
  1.0 0.0 copy-start.1
  1.0 1.0 %copy-done.1 = bf16[2,128,640]{2,1,0:T(8,128)(2,1)S(1)} copy-done((bf16[2,128,640]{2,1,0:T(8,128)(2,1)S(1)}, bf16[2,128,640]{2,1,0:T(8,128)(2,1)}, u32[]{:S(2)}) %copy-start.1) | copy-done | bytes 327704
  2.0 0.0 copy-start.2
  2.0 0.8 %copy-done.2 = bf16[2,128,128]{2,1,0:T(8,128)(2,1)S(1)} copy-done((bf16[2,128,128]{2,1,0:T(8,128)(2,1)S(1)}, bf16[2,128,128]{2,1,0:T(8,128)(2,1)}, u32[]{:S(2)}) %copy-start.2) | copy-done | bytes 65560
  2.9 66.2 %shard_map.37 = bf16[32,64,128]{2,1,0:T(8,128)(2,1)S(1)} custom-call(bf16[64,32,128]{2,1,0:T(8,128)(2,1)S(1)} %copy-done, bf16[2,128,640]{2,1,0:T(8,128)(2,1)S(1)} %copy-done.1, bf16[2,128,128]{2,1,0:T(8,128)(2,1)S(1)} %copy-done.2), custom_call_target="tpu_custom_call" | custom-call | tf_op jit(solution)/shard_map/pallas_call | solution.py:335
  69.1 1.1 %copy.4 = bf16[64,32,128]{2,1,0:T(8,128)(2,1)} copy(bf16[64,32,128]{2,0,1:T(8,128)(2,1)S(1)} %bitcast.1) | data formatting | bytes 1048576 | tf_op jit(solution)/shard_map/transpose | solution.py:376
Async XLA Ops:
  0.0 1.0 %copy-start = (bf16[64,32,128]{2,1,0:T(8,128)(2,1)S(1)}, bf16[64,32,128]{2,1,0:T(8,128)(2,1)}, u32[]{:S(2)}) copy-start(bf16[64,32,128]{2,1,0:T(8,128)(2,1)} %pair_ref.1) | copy-start | bytes 1572868
  1.0 1.0 %copy-start.1 = (bf16[2,128,640]{2,1,0:T(8,128)(2,1)S(1)}, bf16[2,128,640]{2,1,0:T(8,128)(2,1)}, u32[]{:S(2)}) copy-start(bf16[2,128,640]{2,1,0:T(8,128)(2,1)} %proj_ref.1) | copy-start | bytes 983044
  2.0 0.8 %copy-start.2 = (bf16[2,128,128]{2,1,0:T(8,128)(2,1)S(1)}, bf16[2,128,128]{2,1,0:T(8,128)(2,1)}, u32[]{:S(2)}) copy-start(bf16[2,128,128]{2,1,0:T(8,128)(2,1)} %out_proj_ref.1) | copy-start | bytes 196612

commit v2 on v1

--- a/solution.py
+++ b/solution.py
@@ -29,10 +29,13 @@
 
 
 def kernel(
+    pair_hbm,
+    proj_hbm,
+    out_proj_hbm,
+    out_ref,
     pair_ref,
     proj_ref,
     out_proj_ref,
-    out_ref,
     proj_t,
     out_proj_t,
     state,
@@ -63,6 +66,7 @@
     half_recv_sem,
     mixed_send_sem,
     mixed_recv_sem,
+    load_sem,
 ):
     r = lax.axis_index("row")
     col = lax.axis_index("col")
@@ -70,36 +74,46 @@
     core = col % 2
     chip = r * 8 + q
 
-    def device(dest_r, dest_q):
-        return (dest_r, dest_q * 2 + core)
-
+    def around(place):
+        return [lax.rem(place // 4 + d // 4, 2) * 4 + lax.rem(place % 4 + d % 4, 4) for d in range(8)]
+
+    rs, qs = around(r), around(q)
+    cols = [dest_q * 2 + core for dest_q in qs]
     sibling = (r, q * 2 + 1 - core)
+    others = [(d // 8, d % 8) for d in sorted(range(1,64), key=lambda e: (e * 7919) % 1009)]
+
+    loads = [
+        pltpu.make_async_copy(src, dst, load_sem.at[i])
+        for i, (src, dst) in enumerate(
+            ((pair_hbm, pair_ref), (proj_hbm, proj_ref), (out_proj_hbm, out_proj_ref))
+        )
+    ]
+    for load in loads:
+        load.start()
 
     barrier = pltpu.get_barrier_semaphore()
 
-    def greet(d, carry):
-        other = lax.rem(chip + d, 64)
-        pl.semaphore_signal(barrier, inc=1, device_id=device(other // 8, other % 8), device_id_type=MESH)
-        return carry
-
-    lax.fori_loop(1, 64, greet, 0)
+    for dr, dq in others:
+        pl.semaphore_signal(barrier, inc=1, device_id=(rs[dr], cols[dq]), device_id_type=MESH)
     pl.semaphore_signal(barrier, inc=1, device_id=sibling, device_id_type=MESH)
 
-    for u in range(2):
-        proj_t[u] = proj_ref[u].T
-        out_proj_t[u] = out_proj_ref[u].T
-
+    loads[0].wait()
     pair = jnp.swapaxes(pair_ref[...], 0, 1)
     final[...] = pair.reshape(2, 16, 64, 128)
 
-    def load(t, carry):
+    def enter(t, carry):
         for h in range(2):
             block = final[:, 2 * t + h].reshape(128, 128).astype(F32).T
             state[t, :, 128 * h : 128 * h + 128] = block
         normed[t] = normalize(state[t]).astype(BF16)
         return carry
 
-    lax.fori_loop(0, 8, load, 0)
+    lax.fori_loop(0, 8, enter, 0, unroll=8)
+    for load in loads[1:]:
+        load.wait()
+    for u in range(2):
+        proj_t[u] = proj_ref[u].T
+        out_proj_t[u] = out_proj_ref[u].T
 
     def gated(u, first, dest):
         def step(t, carry):
@@ -109,8 +123,8 @@
                 staged[2 * t + h] = value[:, 128 * h : 128 * h + 128]
             return carry
 
-        lax.fori_loop(0, 8, step, 0)
-        dest[u] = jnp.swapaxes(staged[...], 0, 1).reshape(64, 2, 16, 128)
+        lax.fori_loop(0, 8, step, 0, unroll=8)
+        dest[u] = jnp.swapaxes(staged[...], 0, 1).reshape(8, 8, 2, 16, 128)
 
     def gate(u):
         def step(t, carry):
@@ -118,58 +132,51 @@
             gating[t] = sigmoid(p)
             return carry
 
-        lax.fori_loop(0, 8, step, 0)
-
-    def push(src, dst, send_sem, recv_sem, dest_r, dest_q):
-        own = jnp.logical_and(dest_r == r, dest_q == q)
-
-        @pl.when(own)
-        def _():
-            pltpu.make_async_copy(src, dst, recv_sem).start()
-
-        @pl.when(jnp.logical_not(own))
-        def _():
-            pltpu.make_async_remote_copy(
-                src_ref=src,
-                dst_ref=dst,
-                send_sem=send_sem,
-                recv_sem=recv_sem,
-                device_id=device(dest_r, dest_q),
-                device_id_type=MESH,
-            ).start()
+        lax.fori_loop(0, 8, step, 0, unroll=8)
+
+    def push(src, dst, send_sem, recv_sem, device):
+        pltpu.make_async_remote_copy(
+            src_ref=src,
+            dst_ref=dst,
+            send_sem=send_sem,
+            recv_sem=recv_sem,
+            device_id=device,
+            device_id_type=MESH,
+        ).start()
 
     def send_all_left(u):
         slot = recv_left.at[0, r, q] if u == 0 else recv_left.at[1, q, r]
-
-        def step(d, carry):
-            other = lax.rem(chip + 37 * d, 64)
-            push(send_left.at[u, other], slot, left_send_sem.at[u], left_recv_sem.at[u], other // 8, other % 8)
-            return carry
-
-        lax.fori_loop(0, 64, step, 0)
+        pltpu.make_async_copy(send_left.at[u, r, q], slot, left_recv_sem.at[u]).start()
+        for dr, dq in others:
+            push(
+                send_left.at[u, rs[dr], qs[dq]],
+                slot,
+                left_send_sem.at[u],
+                left_recv_sem.at[u],
+                (rs[dr], cols[dq]),
+            )
 
     def send_all_right(u):
         slot = recv_right.at[0, r, q] if u == 0 else recv_right.at[1, q, r]
         mine = r // 2 if u == 0 else q // 2
-
-        def step(d, carry):
-            group = lax.rem(mine + 4 - d // 16, 4)
-            one, eight = (d // 8) % 2, d % 8
-            if u == 0:
-                dest_r, dest_q = group * 2 + (one + r) % 2, (eight + q) % 8
-            else:
-                dest_r, dest_q = (eight + r) % 8, group * 2 + (one + q) % 2
-            push(
-                send_right.at[u, dest_r * 8 + dest_q],
-                slot,
-                right_send_sem.at[u],
-                right_recv_sem.at[u, mine],
-                dest_r,
-                dest_q,
-            )
-            return carry
-
-        lax.fori_loop(0, 64, step, 0)
+        recv_sem = right_recv_sem.at[u, mine]
+        pltpu.make_async_copy(send_right.at[u, r, q], slot, recv_sem).start()
+        for t in range(4):
+            pair = lax.rem(mine + 4 - t, 4) * 2
+            first = r if u == 0 else q
+            near = [pair + lax.rem(first + one, 2) for one in range(2)]
+            for one in range(2):
+                for d in range(8):
+                    if t == 0 and one == 0 and d == 0:
+                        continue
+                    dest_r, dest_q = (near[one], qs[d]) if u == 0 else (rs[d], near[one])
+                    push(
+                        send_right.at[u, dest_r, dest_q],
+                        slot,
+                        right_send_sem.at[u],
+                        recv_sem,
+                        (dest_r, dest_q * 2 + core),
+                    )
 
     def give_back(u, group, c, value):
         for qq in range(2):
@@ -181,19 +188,30 @@
                 send_mixed[u, 2 * group + qq, 2 * m + 1, c] = second
 
     def send_back(u, group):
-        def step(d, carry):
-            dest_q, dest_r = 2 * group + d // 8, (r + d) % 8
-            push(
-                send_mixed.at[u, dest_q, dest_r],
-                recv_mixed.at[u, chip],
-                mixed_send_sem.at[u],
-                mixed_recv_sem.at[u],
-                dest_r,
-                dest_q,
-            )
-            return carry
-
-        lax.fori_loop(0, 16, step, 0)
+        slot = recv_mixed.at[u, chip]
+        for one in range(2):
+            dest_q = 2 * group + one
+            dest_col = dest_q * 2 + core
+            here = dest_q == q
+
+            @pl.when(here)
+            def _():
+                pltpu.make_async_copy(send_mixed.at[u, dest_q, r], slot, mixed_recv_sem.at[u]).start()
+
+            @pl.when(jnp.logical_not(here))
+            def _():
+                push(
+                    send_mixed.at[u, dest_q, r], slot, mixed_send_sem.at[u], mixed_recv_sem.at[u], (r, dest_col)
+                )
+
+            for d in range(1, 8):
+                push(
+                    send_mixed.at[u, dest_q, rs[d]],
+                    slot,
+                    mixed_send_sem.at[u],
+                    mixed_recv_sem.at[u],
+                    (rs[d], dest_col),
+                )
 
     def wait_all(ref, sem):
         pltpu.make_async_copy(ref, ref, sem).wait()
@@ -303,7 +321,7 @@
                     final[:, 2 * t + h] = block.reshape(2, 64, 128)
             return carry
 
-        lax.fori_loop(0, 8, step, 0)
+        lax.fori_loop(0, 8, step, 0, unroll=8)
 
     gated(0, 0, send_left)
     pl.semaphore_wait(barrier, 64)
@@ -323,10 +341,10 @@
     out_ref[...] = final[...].reshape(32, 64, 128)
 
     for u in range(2):
-        sent = pl.ds(0, 63)
-        wait_all(send_left.at[u, sent], left_send_sem.at[u])
-        wait_all(send_right.at[u, sent], right_send_sem.at[u])
-        wait_all(recv_mixed.at[u, sent], mixed_send_sem.at[u])
+        sent = recv_mixed.at[u, pl.ds(0, 63)]
+        wait_all(sent, left_send_sem.at[u])
+        wait_all(sent, right_send_sem.at[u])
+        wait_all(sent, mixed_send_sem.at[u])
 
 
 def shards(pair_state, proj_weight, out_weight):
@@ -335,9 +353,12 @@
     out = pl.pallas_call(
         kernel,
         out_shape=jax.ShapeDtypeStruct((32, 64, 128), BF16),
-        in_specs=[vmem] * 3,
+        in_specs=[pl.BlockSpec(memory_space=pl.ANY)] * 3,
         out_specs=vmem,
         scratch_shapes=[
+            pltpu.VMEM((64, 32, 128), BF16),
+            pltpu.VMEM((2, 128, 640), BF16),
+            pltpu.VMEM((2, 128, 128), BF16),
             pltpu.VMEM((2, 640, 128), BF16),
             pltpu.VMEM((2, 128, 128), BF16),
             pltpu.VMEM((8, 128, 256), F32),
@@ -349,8 +370,8 @@
             pltpu.VMEM((2, 2, 8, 16, 512), BF16),
             pltpu.VMEM((2, 8, 2, 2, 16, 512), BF16),
             pltpu.VMEM((2, 2, 2, 2, 32, 512), F32),
-            pltpu.VMEM((2, 64, 2, 16, 128), BF16),
-            pltpu.VMEM((2, 64, 2, 16, 128), BF16),
+            pltpu.VMEM((2, 8, 8, 2, 16, 128), BF16),
+            pltpu.VMEM((2, 8, 8, 2, 16, 128), BF16),
             pltpu.VMEM((2, 8, 8, 2, 16, 128), BF16),
             pltpu.VMEM((2, 8, 8, 2, 16, 128), BF16),
             pltpu.VMEM((8, 8, 2, 16, 128), BF16),
@@ -368,9 +389,10 @@
             dma((4,)),
             dma((2,)),
             dma((2,)),
+            dma((3,)),
         ],
         compiler_params=pltpu.CompilerParams(
-            collective_id=0, has_side_effects=True, vmem_limit_bytes=48 * 2**20
+            collective_id=0, has_side_effects=True, vmem_limit_bytes=56 * 2**20
         ),
     )(pair_state, proj_weight, out_weight)
     return jnp.transpose(out, (1, 0, 2))

time: 71.3 us -> 64.3 us (0.902)
  Pallas kernels: 66.2 us -> 61.3 us
  local copies, waits for them, and re-layouts: 3.99 us -> 2.18 us
    pallas_call x1, Pallas kernels: 66.2 us -> 61.3 us  [shards(): pl.pallas_call(kernel, out_shape=jax.ShapeDtypeStruct((32, 64, 128), BF16...]
    unnamed x6 -> x0, local copies, waits for them, and re-layouts: 2.85 us -> none
    transpose x1, local copies, waits for them, and re-layouts: 1.14 us -> 2.18 us  [shards(): return jnp.transpose(out, (1, 0, 2))]
where the time goes in v2:
time: 64.3 us; the launch traced here: 63.5 us
  Pallas kernels  61.3 us (95%)
  local copies, waits for them, and re-layouts  2.18 us (3%)
    pallas_call x1, Pallas kernels, shards(): pl.pallas_call(kernel, out_shape=jax.ShapeDtypeStruct((32, 64, 128), BF16...  61.3 us
    transpose x1, local copies, waits for them, and re-layouts, shards(): return jnp.transpose(out, (1, 0, 2))  2.18 us

profile of v2, /device:TPU:0, one launch (start us, length us, event | category | flops | bytes accessed | tf_op | source)
XLA Modules:
  0.0 63.5 jit_solution(15911167786121021926)
XLA Ops:
  0.0 61.3 %shard_map.37 = bf16[32,64,128]{2,1,0:T(8,128)(2,1)} custom-call(bf16[64,32,128]{2,1,0:T(8,128)(2,1)} %pair_hbm.1, bf16[2,128,640]{2,1,0:T(8,128)(2,1)} %proj_hbm.1, bf16[2,128,128]{2,1,0:T(8,128)(2,1)} %out_proj_hbm.1), custom_call_target="tpu_custom_call" | custom-call | tf_op jit(solution)/shard_map/pallas_call | solution.py:353
  61.3 2.2 %copy.4 = bf16[64,32,128]{2,1,0:T(8,128)(2,1)} copy(bf16[64,32,128]{2,0,1:T(8,128)(2,1)} %bitcast.1) | data formatting | bytes 1048576 | tf_op jit(solution)/shard_map/transpose | solution.py:398

commit v3 on v2

--- a/solution.py
+++ b/solution.py
@@ -48,14 +48,18 @@
     left_op1,
     partial,
     send_left,
+    send_left1,
     send_right,
     recv_left,
+    recv_left1,
     recv_right,
     sibling_left,
     half_send,
     half_recv,
-    send_mixed,
-    recv_mixed,
+    send_half,
+    recv_half,
+    send_whole,
+    recv_whole,
     left_send_sem,
     left_recv_sem,
     right_send_sem,
@@ -115,16 +119,23 @@
         proj_t[u] = proj_ref[u].T
         out_proj_t[u] = out_proj_ref[u].T
 
-    def gated(u, first, dest):
-        def step(t, carry):
+    def gated(u, first, tiles):
+        for t in tiles:
             p = jnp.dot(proj_t[u, first : first + 256], normed[t], preferred_element_type=F32)
-            value = (sigmoid(p[:128]) * p[128:]).astype(BF16)
+            value = sigmoid(p[:128]) * p[128:]
             for h in range(2):
-                staged[2 * t + h] = value[:, 128 * h : 128 * h + 128]
-            return carry
-
-        lax.fori_loop(0, 8, step, 0, unroll=8)
-        dest[u] = jnp.swapaxes(staged[...], 0, 1).reshape(8, 8, 2, 16, 128)
+                staged[2 * t + h] = value[:, 128 * h : 128 * h + 128].astype(BF16)
+        return jnp.swapaxes(staged[2 * tiles[0] : 2 * tiles[-1] + 2], 0, 1)
+
+    def whole_left(u):
+        send_left[...] = gated(u, 0, range(8)).reshape(8, 8, 2, 16, 128)
+
+    def half_left(half):
+        value = gated(1, 0, range(4 * half, 4 * half + 4)).astype(F32)
+        send_left1[half] = value.reshape(8, 8, 16, 128).astype(BF16)
+
+    def whole_right(u):
+        send_right[u] = gated(u, 256, range(8)).reshape(8, 8, 2, 16, 128)
 
     def gate(u):
         def step(t, carry):
@@ -144,17 +155,18 @@
             device_id_type=MESH,
         ).start()
 
-    def send_all_left(u):
-        slot = recv_left.at[0, r, q] if u == 0 else recv_left.at[1, q, r]
-        pltpu.make_async_copy(send_left.at[u, r, q], slot, left_recv_sem.at[u]).start()
+    def send_all_left(src, slot, send_sem, recv_sem):
+        pltpu.make_async_copy(src.at[r, q], slot, recv_sem).start()
         for dr, dq in others:
-            push(
-                send_left.at[u, rs[dr], qs[dq]],
-                slot,
-                left_send_sem.at[u],
-                left_recv_sem.at[u],
-                (rs[dr], cols[dq]),
-            )
+            push(src.at[rs[dr], qs[dq]], slot, send_sem, recv_sem, (rs[dr], cols[dq]))
+
+    def send_whole_left():
+        send_all_left(send_left, recv_left.at[r, q], left_send_sem.at[2], left_recv_sem.at[2])
+
+    def send_half_left(half):
+        send_all_left(
+            send_left1.at[half], recv_left1.at[half, q, r], left_send_sem.at[half], left_recv_sem.at[half]
+        )
 
     def send_all_right(u):
         slot = recv_right.at[0, r, q] if u == 0 else recv_right.at[1, q, r]
@@ -178,17 +190,28 @@
                         (dest_r, dest_q * 2 + core),
                     )
 
-    def give_back(u, group, c, value):
-        for qq in range(2):
+    def give_halves(group, values):
+        for half in range(2):
+            for one in range(2):
+                low, high = (
+                    jnp.concatenate([v[one, at : at + 8] for v in values], axis=0).astype(BF16)
+                    for at in (8 * half, 8 * half + 16)
+                )
+                for m in range(4):
+                    lanes = slice(128 * m, 128 * m + 128)
+                    first, second = interleave(low[:, lanes], high[:, lanes])
+                    send_half[half, 2 * group + one, 2 * m] = first
+                    send_half[half, 2 * group + one, 2 * m + 1] = second
+
+    def give_whole(group, c, value):
+        for one in range(2):
             for m in range(4):
-                lower = value[qq, :16, 128 * m : 128 * m + 128]
-                upper = value[qq, 16:, 128 * m : 128 * m + 128]
-                first, second = interleave(lower, upper)
-                send_mixed[u, 2 * group + qq, 2 * m, c] = first
-                send_mixed[u, 2 * group + qq, 2 * m + 1, c] = second
-
-    def send_back(u, group):
-        slot = recv_mixed.at[u, chip]
+                lanes = slice(128 * m, 128 * m + 128)
+                first, second = interleave(value[one, :16, lanes], value[one, 16:, lanes])
+                send_whole[2 * group + one, 2 * m, c] = first
+                send_whole[2 * group + one, 2 * m + 1, c] = second
+
+    def send_back(src, slot, send_sem, recv_sem, group):
         for one in range(2):
             dest_q = 2 * group + one
             dest_col = dest_q * 2 + core
@@ -196,31 +219,31 @@
 
             @pl.when(here)
             def _():
-                pltpu.make_async_copy(send_mixed.at[u, dest_q, r], slot, mixed_recv_sem.at[u]).start()
+                pltpu.make_async_copy(src.at[dest_q, r], slot, recv_sem).start()
 
             @pl.when(jnp.logical_not(here))
             def _():
-                push(
-                    send_mixed.at[u, dest_q, r], slot, mixed_send_sem.at[u], mixed_recv_sem.at[u], (r, dest_col)
-                )
+                push(src.at[dest_q, r], slot, send_sem, recv_sem, (r, dest_col))
 
             for d in range(1, 8):
-                push(
-                    send_mixed.at[u, dest_q, rs[d]],
-                    slot,
-                    mixed_send_sem.at[u],
-                    mixed_recv_sem.at[u],
-                    (rs[d], dest_col),
-                )
+                push(src.at[dest_q, rs[d]], slot, send_sem, recv_sem, (rs[d], dest_col))
+
+    def send_half_back(half, group):
+        send_back(
+            send_half.at[half], recv_half.at[half, chip], mixed_send_sem.at[half], mixed_recv_sem.at[half], group
+        )
+
+    def send_whole_back(group):
+        send_back(send_whole, recv_whole.at[chip], mixed_send_sem.at[2], mixed_recv_sem.at[2], group)
 
     def wait_all(ref, sem):
         pltpu.make_async_copy(ref, ref, sem).wait()
 
     def outgoing():
-        wait_all(recv_left.at[0], left_recv_sem.at[0])
+        wait_all(recv_left, left_recv_sem.at[2])
         for c in range(2):
             for m in range(4):
-                first, second = interleave(recv_left[0, 2 * m, :, c], recv_left[0, 2 * m + 1, :, c])
+                first, second = interleave(recv_left[2 * m, :, c], recv_left[2 * m + 1, :, c])
                 left_op0[c, 0, :, :, 128 * m : 128 * m + 128] = first
                 left_op0[c, 1, :, :, 128 * m : 128 * m + 128] = second
 
@@ -237,10 +260,9 @@
         def finish_group(t):
             group = lax.rem(r // 2 + t, 4)
             half_copy(t).wait_recv()
-            for c in range(2):
-                total = partial[t % 2, c, :, core] + half_recv[t, c].astype(F32)
-                give_back(0, group, c, total.astype(BF16))
-            send_back(0, group)
+            totals = [partial[t % 2, c, :, core] + half_recv[t, c].astype(F32) for c in range(2)]
+            give_halves(group, totals)
+            send_half_back(0, group)
 
         for t in range(4):
             group = lax.rem(r // 2 + t, 4)
@@ -258,30 +280,37 @@
                 finish_group(t - 1)
         finish_group(3)
         for t in range(4):
+            send_half_back(1, lax.rem(r // 2 + t, 4))
+        for t in range(4):
             half_copy(t).wait_send()
 
     def incoming():
-        wait_all(recv_left.at[1], left_recv_sem.at[1])
-        swap = pltpu.make_async_remote_copy(
-            src_ref=recv_left.at[1],
-            dst_ref=sibling_left,
-            send_sem=sib_send_sem,
-            recv_sem=sib_recv_sem,
-            device_id=sibling,
-            device_id_type=MESH,
-        )
-        swap.start()
-
-        def arrange(blocks, which):
-            for c in range(2):
-                for m in range(4):
-                    first, second = interleave(blocks[:, 2 * m, c], blocks[:, 2 * m + 1, c])
-                    left_op1[c, :, which, 0, :, 128 * m : 128 * m + 128] = first
-                    left_op1[c, :, which, 1, :, 128 * m : 128 * m + 128] = second
-
-        arrange(recv_left.at[1], core)
-        swap.wait_recv()
-        arrange(sibling_left, 1 - core)
+        def arrange(ref, half, which):
+            for m in range(4):
+                pieces = interleave(ref[half, :, 2 * m], ref[half, :, 2 * m + 1])
+                for part in range(2):
+                    for c in range(2):
+                        left_op1[c, :, which, part, 8 * half : 8 * half + 8, 128 * m : 128 * m + 128] = pieces[
+                            part
+                        ][:, 8 * c : 8 * c + 8]
+
+        swaps = []
+        for half in range(2):
+            wait_all(recv_left1.at[half], left_recv_sem.at[half])
+            swap = pltpu.make_async_remote_copy(
+                src_ref=recv_left1.at[half],
+                dst_ref=sibling_left.at[half],
+                send_sem=sib_send_sem.at[half],
+                recv_sem=sib_recv_sem.at[half],
+                device_id=sibling,
+                device_id_type=MESH,
+            )
+            swap.start()
+            swaps.append(swap)
+            arrange(recv_left1, half, core)
+        for half in range(2):
+            swaps[half].wait_recv()
+            arrange(sibling_left, half, 1 - core)
 
         for t in range(4):
             group = lax.rem(q // 2 + t, 4)
@@ -296,55 +325,59 @@
                 product = lax.dot_general(
                     right, left_op1[c].reshape(512, 512), (((1,), (1,)), ((), ())), preferred_element_type=F32
                 )
-                give_back(1, group, c, product.astype(BF16).reshape(2, 32, 512))
-            send_back(1, group)
-        swap.wait_send()
-
-    def absorb(u):
-        wait_all(recv_mixed.at[u], mixed_recv_sem.at[u])
-        mixed = recv_mixed[u].reshape(128, 16, 128).astype(F32)
-        norm = jnp.swapaxes(normalize(mixed).astype(BF16), 0, 1)
+                give_whole(group, c, product.astype(BF16).reshape(2, 32, 512))
+            send_whole_back(group)
+        for swap in swaps:
+            swap.wait_send()
+
+    def absorb_half(half):
+        wait_all(recv_half.at[half], mixed_recv_sem.at[half])
+        norm = normalize(recv_half[half].astype(F32).reshape(128, 8, 128))
+        norm = jnp.swapaxes(norm, 0, 1).astype(BF16)
+        for t in range(4 * half, 4 * half + 4):
+            for h in range(2):
+                mixnorm[t, :, 128 * h : 128 * h + 128] = norm[2 * t + h - 8 * half]
+            output = jnp.dot(out_proj_t[0], mixnorm[t], preferred_element_type=F32)
+            updated = (state[t] + gating[t] * output).astype(BF16).astype(F32)
+            state[t] = updated
+            normed[t] = normalize(updated).astype(BF16)
+
+    def absorb_whole():
+        wait_all(recv_whole, mixed_recv_sem.at[2])
+        norm = normalize(recv_whole[...].reshape(128, 16, 128).astype(F32))
+        norm = jnp.swapaxes(norm.astype(BF16), 0, 1)
         for t in range(8):
             for h in range(2):
                 mixnorm[t, :, 128 * h : 128 * h + 128] = norm[2 * t + h]
-
-        def step(t, carry):
-            output = jnp.dot(out_proj_t[u], mixnorm[t], preferred_element_type=F32)
+            output = jnp.dot(out_proj_t[1], mixnorm[t], preferred_element_type=F32)
             updated = state[t] + gating[t] * output
-            if u == 0:
-                updated = updated.astype(BF16).astype(F32)
-                state[t] = updated
-                normed[t] = normalize(updated).astype(BF16)
-            else:
-                for h in range(2):
-                    block = updated[:, 128 * h : 128 * h + 128].T.astype(BF16)
-                    final[:, 2 * t + h] = block.reshape(2, 64, 128)
-            return carry
-
-        lax.fori_loop(0, 8, step, 0, unroll=8)
-
-    gated(0, 0, send_left)
+            for h in range(2):
+                block = updated[:, 128 * h : 128 * h + 128].T.astype(BF16)
+                final[:, 2 * t + h] = block.reshape(2, 64, 128)
+
+    whole_left(0)
     pl.semaphore_wait(barrier, 64)
-    send_all_left(0)
-    gated(0, 256, send_right)
+    send_whole_left()
+    whole_right(0)
     send_all_right(0)
     gate(0)
     outgoing()
-    absorb(0)
-    gated(1, 0, send_left)
-    send_all_left(1)
-    gated(1, 256, send_right)
+    for half in range(2):
+        absorb_half(half)
+        half_left(half)
+        send_half_left(half)
+    whole_right(1)
     send_all_right(1)
     gate(1)
     incoming()
-    absorb(1)
+    absorb_whole()
     out_ref[...] = final[...].reshape(32, 64, 128)
 
-    for u in range(2):
-        sent = recv_mixed.at[u, pl.ds(0, 63)]
-        wait_all(sent, left_send_sem.at[u])
-        wait_all(sent, right_send_sem.at[u])
-        wait_all(sent, mixed_send_sem.at[u])
+    for half in range(2):
+        wait_all(recv_half.at[half, pl.ds(0, 63)], left_send_sem.at[half])
+        wait_all(recv_half.at[half, pl.ds(0, 63)], mixed_send_sem.at[half])
+    for sem in (left_send_sem.at[2], right_send_sem.at[0], right_send_sem.at[1], mixed_send_sem.at[2]):
+        wait_all(recv_whole.at[pl.ds(0, 63)], sem)
 
 
 def shards(pair_state, proj_weight, out_weight):
@@ -370,25 +403,29 @@
             pltpu.VMEM((2, 2, 8, 16, 512), BF16),
             pltpu.VMEM((2, 8, 2, 2, 16, 512), BF16),
             pltpu.VMEM((2, 2, 2, 2, 32, 512), F32),
-            pltpu.VMEM((2, 8, 8, 2, 16, 128), BF16),
-            pltpu.VMEM((2, 8, 8, 2, 16, 128), BF16),
-            pltpu.VMEM((2, 8, 8, 2, 16, 128), BF16),
+            pltpu.VMEM((8, 8, 2, 16, 128), BF16),
+            pltpu.VMEM((2, 8, 8, 16, 128), BF16),
             pltpu.VMEM((2, 8, 8, 2, 16, 128), BF16),
             pltpu.VMEM((8, 8, 2, 16, 128), BF16),
+            pltpu.VMEM((2, 8, 8, 16, 128), BF16),
+            pltpu.VMEM((2, 8, 8, 2, 16, 128), BF16),
+            pltpu.VMEM((2, 8, 8, 16, 128), BF16),
             pltpu.VMEM((4, 2, 2, 32, 512), BF16),
             pltpu.VMEM((4, 2, 2, 32, 512), BF16),
-            pltpu.VMEM((2, 8, 8, 2, 16, 128), BF16),
-            pltpu.VMEM((2, 64, 2, 16, 128), BF16),
+            pltpu.VMEM((2, 8, 8, 16, 128), BF16),
+            pltpu.VMEM((2, 64, 16, 128), BF16),
+            pltpu.VMEM((8, 8, 2, 16, 128), BF16),
+            pltpu.VMEM((64, 2, 16, 128), BF16),
+            dma((3,)),
+            dma((3,)),
+            dma((2,)),
+            dma((2, 4)),
             dma((2,)),
             dma((2,)),
-            dma((2,)),
-            dma((2, 4)),
-            dma,
-            dma,
             dma((4,)),
             dma((4,)),
-            dma((2,)),
-            dma((2,)),
+            dma((3,)),
+            dma((3,)),
             dma((3,)),
         ],
         compiler_params=pltpu.CompilerParams(

time: 64.3 us -> 62.8 us (0.977)
  Pallas kernels: 61.3 us -> 59.8 us
    pallas_call x1, Pallas kernels: 61.3 us -> 59.8 us  [shards(): pl.pallas_call(kernel, out_shape=jax.ShapeDtypeStruct((32, 64, 128), BF16...]
where the time goes in v3:
time: 62.8 us; the launch traced here: 62 us
  Pallas kernels  59.8 us (95%)
  local copies, waits for them, and re-layouts  2.18 us (3%)
    pallas_call x1, Pallas kernels, shards(): pl.pallas_call(kernel, out_shape=jax.ShapeDtypeStruct((32, 64, 128), BF16...  59.8 us
    transpose x1, local copies, waits for them, and re-layouts, shards(): return jnp.transpose(out, (1, 0, 2))  2.18 us

profile of v3, /device:TPU:0, one launch (start us, length us, event | category | flops | bytes accessed | tf_op | source)
XLA Modules:
  0.0 62.0 jit_solution(10609237864695290942)
XLA Ops:
  0.0 59.8 %shard_map.37 = bf16[32,64,128]{2,1,0:T(8,128)(2,1)} custom-call(bf16[64,32,128]{2,1,0:T(8,128)(2,1)} %pair_hbm.1, bf16[2,128,640]{2,1,0:T(8,128)(2,1)} %proj_hbm.1, bf16[2,128,128]{2,1,0:T(8,128)(2,1)} %out_proj_hbm.1), custom_call_target="tpu_custom_call" | custom-call | tf_op jit(solution)/shard_map/pallas_call | solution.py:386
  59.8 2.2 %copy.4 = bf16[64,32,128]{2,1,0:T(8,128)(2,1)} copy(bf16[64,32,128]{2,0,1:T(8,128)(2,1)} %bitcast.1) | data formatting | bytes 1048576 | tf_op jit(solution)/shard_map/transpose | solution.py:435

commit v4 on v3

--- a/solution.py
+++ b/solution.py
@@ -71,6 +71,7 @@
     mixed_send_sem,
     mixed_recv_sem,
     load_sem,
+    out_sem,
 ):
     r = lax.axis_index("row")
     col = lax.axis_index("col")
@@ -82,6 +83,15 @@
         return [lax.rem(place // 4 + d // 4, 2) * 4 + lax.rem(place % 4 + d % 4, 4) for d in range(8)]
 
     rs, qs = around(r), around(q)
+
+    def group_of(place):
+        return place // 4 * 2 + place % 2
+
+    def place_of(group, one):
+        return group // 2 * 4 + group % 2 + 2 * one
+
+    start = lax.rem(r % 4 + q // 4 * 2 + q % 4, 4)
+    turns = [lax.rem(start + t, 4) for t in range(4)]
     cols = [dest_q * 2 + core for dest_q in qs]
     sibling = (r, q * 2 + 1 - core)
     others = [(d // 8, d % 8) for d in sorted(range(1,64), key=lambda e: (e * 7919) % 1009)]
@@ -169,26 +179,29 @@
         )
 
     def send_all_right(u):
-        slot = recv_right.at[0, r, q] if u == 0 else recv_right.at[1, q, r]
-        mine = r // 2 if u == 0 else q // 2
-        recv_sem = right_recv_sem.at[u, mine]
-        pltpu.make_async_copy(send_right.at[u, r, q], slot, recv_sem).start()
+        place, other = (r, q) if u == 0 else (q, r)
+        mine = group_of(place)
+        slot = recv_right.at[u, mine, place % 4 // 2, other]
+        send_sem, recv_sem = right_send_sem.at[u], right_recv_sem.at[u, mine]
         for t in range(4):
-            pair = lax.rem(mine + 4 - t, 4) * 2
-            first = r if u == 0 else q
-            near = [pair + lax.rem(first + one, 2) for one in range(2)]
-            for one in range(2):
+            for dz in range(2):
+                dest_rz = rs[4 * dz] // 4 * 4
                 for d in range(8):
-                    if t == 0 and one == 0 and d == 0:
+                    dest_q = qs[d]
+                    dest_r = dest_rz + lax.rem(mine + 16 - t - dest_q // 4 * 2 - dest_q % 4, 4)
+                    src = send_right.at[u, dest_r, dest_q]
+                    if dz or d:
+                        push(src, slot, send_sem, recv_sem, (dest_r, cols[d]))
                         continue
-                    dest_r, dest_q = (near[one], qs[d]) if u == 0 else (rs[d], near[one])
-                    push(
-                        send_right.at[u, dest_r, dest_q],
-                        slot,
-                        right_send_sem.at[u],
-                        recv_sem,
-                        (dest_r, dest_q * 2 + core),
-                    )
+                    here = dest_r == r
+
+                    @pl.when(here)
+                    def _():
+                        pltpu.make_async_copy(src, slot, recv_sem).start()
+
+                    @pl.when(jnp.logical_not(here))
+                    def _():
+                        push(src, slot, send_sem, recv_sem, (dest_r, cols[d]))
 
     def give_halves(group, values):
         for half in range(2):
@@ -200,20 +213,20 @@
                 for m in range(4):
                     lanes = slice(128 * m, 128 * m + 128)
                     first, second = interleave(low[:, lanes], high[:, lanes])
-                    send_half[half, 2 * group + one, 2 * m] = first
-                    send_half[half, 2 * group + one, 2 * m + 1] = second
+                    send_half[half, place_of(group, one), 2 * m] = first
+                    send_half[half, place_of(group, one), 2 * m + 1] = second
 
     def give_whole(group, c, value):
         for one in range(2):
             for m in range(4):
                 lanes = slice(128 * m, 128 * m + 128)
                 first, second = interleave(value[one, :16, lanes], value[one, 16:, lanes])
-                send_whole[2 * group + one, 2 * m, c] = first
-                send_whole[2 * group + one, 2 * m + 1, c] = second
+                send_whole[place_of(group, one), 2 * m, c] = first
+                send_whole[place_of(group, one), 2 * m + 1, c] = second
 
     def send_back(src, slot, send_sem, recv_sem, group):
         for one in range(2):
-            dest_q = 2 * group + one
+            dest_q = place_of(group, one)
             dest_col = dest_q * 2 + core
             here = dest_q == q
 
@@ -258,17 +271,17 @@
             )
 
         def finish_group(t):
-            group = lax.rem(r // 2 + t, 4)
+            group = turns[t]
             half_copy(t).wait_recv()
             totals = [partial[t % 2, c, :, core] + half_recv[t, c].astype(F32) for c in range(2)]
             give_halves(group, totals)
             send_half_back(0, group)
 
         for t in range(4):
-            group = lax.rem(r // 2 + t, 4)
-            wait_all(recv_right.at[0, pl.ds(2 * group, 2)], right_recv_sem.at[0, group])
+            group = turns[t]
+            wait_all(recv_right.at[0, group], right_recv_sem.at[0, group])
             for c in range(2):
-                first, second = interleave(recv_right[0, 2 * group, :, c], recv_right[0, 2 * group + 1, :, c])
+                first, second = interleave(recv_right[0, group, 0, :, c], recv_right[0, group, 1, :, c])
                 right = jnp.concatenate([first.reshape(128, 128), second.reshape(128, 128)], axis=0)
                 product = lax.dot_general(
                     right, left_op0[c].reshape(256, 512), (((0,), (0,)), ((), ())), preferred_element_type=F32
@@ -280,7 +293,7 @@
                 finish_group(t - 1)
         finish_group(3)
         for t in range(4):
-            send_half_back(1, lax.rem(r // 2 + t, 4))
+            send_half_back(1, turns[t])
         for t in range(4):
             half_copy(t).wait_send()
 
@@ -313,13 +326,13 @@
             arrange(sibling_left, half, 1 - core)
 
         for t in range(4):
-            group = lax.rem(q // 2 + t, 4)
-            wait_all(recv_right.at[1, pl.ds(2 * group, 2)], right_recv_sem.at[1, group])
+            group = turns[t]
+            wait_all(recv_right.at[1, group], right_recv_sem.at[1, group])
             for c in range(2):
                 columns = []
                 for m in range(4):
-                    even = recv_right[1, pl.ds(2 * group, 2), 2 * m, c]
-                    odd = recv_right[1, pl.ds(2 * group, 2), 2 * m + 1, c]
+                    even = recv_right[1, group, :, 2 * m, c]
+                    odd = recv_right[1, group, :, 2 * m + 1, c]
                     columns.append(jnp.stack(interleave(even, odd), axis=1).reshape(64, 128))
                 right = jnp.concatenate(columns, axis=1)
                 product = lax.dot_general(
@@ -354,6 +367,10 @@
             for h in range(2):
                 block = updated[:, 128 * h : 128 * h + 128].T.astype(BF16)
                 final[:, 2 * t + h] = block.reshape(2, 64, 128)
+            for part in range(2):
+                pltpu.make_async_copy(
+                    final.at[part, pl.ds(2 * t, 2)], out_ref.at[pl.ds(16 * part + 2 * t, 2)], out_sem
+                ).start()
 
     whole_left(0)
     pl.semaphore_wait(barrier, 64)
@@ -371,23 +388,22 @@
     gate(1)
     incoming()
     absorb_whole()
-    out_ref[...] = final[...].reshape(32, 64, 128)
 
     for half in range(2):
         wait_all(recv_half.at[half, pl.ds(0, 63)], left_send_sem.at[half])
         wait_all(recv_half.at[half, pl.ds(0, 63)], mixed_send_sem.at[half])
     for sem in (left_send_sem.at[2], right_send_sem.at[0], right_send_sem.at[1], mixed_send_sem.at[2]):
         wait_all(recv_whole.at[pl.ds(0, 63)], sem)
+    wait_all(out_ref, out_sem)
 
 
 def shards(pair_state, proj_weight, out_weight):
-    vmem = pl.BlockSpec(memory_space=pltpu.VMEM)
     dma = pltpu.SemaphoreType.DMA
     out = pl.pallas_call(
         kernel,
         out_shape=jax.ShapeDtypeStruct((32, 64, 128), BF16),
         in_specs=[pl.BlockSpec(memory_space=pl.ANY)] * 3,
-        out_specs=vmem,
+        out_specs=pl.BlockSpec(memory_space=pl.ANY),
         scratch_shapes=[
             pltpu.VMEM((64, 32, 128), BF16),
             pltpu.VMEM((2, 128, 640), BF16),
@@ -408,7 +424,7 @@
             pltpu.VMEM((2, 8, 8, 2, 16, 128), BF16),
             pltpu.VMEM((8, 8, 2, 16, 128), BF16),
             pltpu.VMEM((2, 8, 8, 16, 128), BF16),
-            pltpu.VMEM((2, 8, 8, 2, 16, 128), BF16),
+            pltpu.VMEM((2, 4, 2, 8, 2, 16, 128), BF16),
             pltpu.VMEM((2, 8, 8, 16, 128), BF16),
             pltpu.VMEM((4, 2, 2, 32, 512), BF16),
             pltpu.VMEM((4, 2, 2, 32, 512), BF16),
@@ -427,6 +443,7 @@
             dma((3,)),
             dma((3,)),
             dma((3,)),
+            dma,
         ],
         compiler_params=pltpu.CompilerParams(
             collective_id=0, has_side_effects=True, vmem_limit_bytes=56 * 2**20

time: 62.8 us -> 60.8 us (0.968); the launches traced: 62 us -> 60.7 us
  Pallas kernels: 59.8 us -> 58.5 us
    pallas_call x1, Pallas kernels: 59.8 us -> 58.5 us  [shards(): pl.pallas_call(kernel, out_shape=jax.ShapeDtypeStruct((32, 64, 128), BF16...]
where the time goes in v4:
time: 60.8 us; the launch traced here: 60.7 us
  Pallas kernels  58.5 us (96%)
  local copies, waits for them, and re-layouts  2.18 us (4%)
    pallas_call x1, Pallas kernels, shards(): pl.pallas_call(kernel, out_shape=jax.ShapeDtypeStruct((32, 64, 128), BF16...  58.5 us
    transpose x1, local copies, waits for them, and re-layouts, shards(): return jnp.transpose(out, (1, 0, 2))  2.18 us

profile of v4, /device:TPU:0, one launch (start us, length us, event | category | flops | bytes accessed | tf_op | source)
XLA Modules:
  0.0 60.7 jit_solution(13586625873301849829)
XLA Ops:
  0.0 58.5 %shard_map.37 = bf16[32,64,128]{2,1,0:T(8,128)(2,1)} custom-call(bf16[64,32,128]{2,1,0:T(8,128)(2,1)} %pair_hbm.1, bf16[2,128,640]{2,1,0:T(8,128)(2,1)} %proj_hbm.1, bf16[2,128,128]{2,1,0:T(8,128)(2,1)} %out_proj_hbm.1), custom_call_target="tpu_custom_call" | custom-call | tf_op jit(solution)/shard_map/pallas_call | solution.py:402
  58.5 2.2 %copy.4 = bf16[64,32,128]{2,1,0:T(8,128)(2,1)} copy(bf16[64,32,128]{2,0,1:T(8,128)(2,1)} %bitcast.1) | data formatting | bytes 1048576 | tf_op jit(solution)/shard_map/transpose | solution.py:452

commit v5 on v4

--- a/solution.py
+++ b/solution.py
@@ -26,6 +26,11 @@
     first = jnp.concatenate([even[..., :64], odd[..., :64]], axis=-1)
     second = jnp.concatenate([even[..., 64:], odd[..., 64:]], axis=-1)
     return first, second
+
+
+def swap_blocks(x, axis):
+    blocks = jnp.split(x, 4, axis=axis)
+    return jnp.concatenate([blocks[0], blocks[2], blocks[1], blocks[3]], axis=axis)
 
 
 def kernel(
@@ -49,10 +54,13 @@
     partial,
     send_left,
     send_left1,
+    send_right0,
     send_right,
     recv_left,
     recv_left1,
+    recv_right0,
     recv_right,
+    right_op,
     sibling_left,
     half_send,
     half_recv,
@@ -63,6 +71,7 @@
     left_send_sem,
     left_recv_sem,
     right_send_sem,
+    right_recv0_sem,
     right_recv_sem,
     sib_send_sem,
     sib_recv_sem,
@@ -92,6 +101,8 @@
 
     start = lax.rem(r % 4 + q // 4 * 2 + q % 4, 4)
     turns = [lax.rem(start + t, 4) for t in range(4)]
+
+    sets = [lax.rem(r + q + t, 2) for t in range(2)]
     cols = [dest_q * 2 + core for dest_q in qs]
     sibling = (r, q * 2 + 1 - core)
     others = [(d // 8, d % 8) for d in sorted(range(1,64), key=lambda e: (e * 7919) % 1009)]
@@ -112,8 +123,11 @@
     pl.semaphore_signal(barrier, inc=1, device_id=sibling, device_id_type=MESH)
 
     loads[0].wait()
-    pair = jnp.swapaxes(pair_ref[...], 0, 1)
-    final[...] = pair.reshape(2, 16, 64, 128)
+    pair = jnp.swapaxes(swap_blocks(pair_ref[...], 0), 0, 1)
+    for half in range(2):
+        for part in range(2):
+            first = 16 * half + 8 * part
+            final[part, 8 * half : 8 * half + 8] = pair[first : first + 8]
 
     def enter(t, carry):
         for h in range(2):
@@ -144,8 +158,16 @@
         value = gated(1, 0, range(4 * half, 4 * half + 4)).astype(F32)
         send_left1[half] = value.reshape(8, 8, 16, 128).astype(BF16)
 
-    def whole_right(u):
-        send_right[u] = gated(u, 256, range(8)).reshape(8, 8, 2, 16, 128)
+    def half_rights():
+        value = gated(0, 256, range(8)).astype(F32)
+        low, high = value[:, :8], value[:, 8:]
+        for half in range(2):
+            lanes = [slice(32 * half + 64 * part, 32 * half + 64 * part + 32) for part in range(2)]
+            pieces = jnp.concatenate([tile[..., at] for tile in (low, high) for at in lanes], axis=-1)
+            send_right0[half] = pieces.reshape(8, 8, 16, 128).astype(BF16)
+
+    def whole_right():
+        send_right[...] = gated(1, 256, range(8)).reshape(8, 8, 2, 16, 128)
 
     def gate(u):
         def step(t, carry):
@@ -165,6 +187,15 @@
             device_id_type=MESH,
         ).start()
 
+    def push_or_keep(here, src, dst, send_sem, recv_sem, device):
+        @pl.when(here)
+        def _():
+            pltpu.make_async_copy(src, dst, recv_sem).start()
+
+        @pl.when(jnp.logical_not(here))
+        def _():
+            push(src, dst, send_sem, recv_sem, device)
+
     def send_all_left(src, slot, send_sem, recv_sem):
         pltpu.make_async_copy(src.at[r, q], slot, recv_sem).start()
         for dr, dq in others:
@@ -178,43 +209,47 @@
             send_left1.at[half], recv_left1.at[half, q, r], left_send_sem.at[half], left_recv_sem.at[half]
         )
 
-    def send_all_right(u):
-        place, other = (r, q) if u == 0 else (q, r)
-        mine = group_of(place)
-        slot = recv_right.at[u, mine, place % 4 // 2, other]
-        send_sem, recv_sem = right_send_sem.at[u], right_recv_sem.at[u, mine]
+    def send_half_right(half):
+        mine = r % 2
+        slot = recv_right0.at[half, mine, r // 2, q]
+        send_sem, recv_sem = right_send_sem.at[half], right_recv0_sem.at[half, mine]
+        for t in range(2):
+            for d in range(32):
+                dest_q = qs[d % 8]
+                dest_r = lax.rem(r // 2 + d // 8, 4) * 2 + lax.rem(mine + t + dest_q, 2)
+                col = cols[d % 8]
+                src = send_right0.at[half, dest_r, dest_q]
+                if d:
+                    push(src, slot, send_sem, recv_sem, (dest_r, col))
+                else:
+                    push_or_keep(dest_r == r, src, slot, send_sem, recv_sem, (dest_r, col))
+
+    def send_whole_right():
+        mine = group_of(q)
+        slot = recv_right.at[mine, q % 4 // 2, r]
+        send_sem, recv_sem = right_send_sem.at[2], right_recv_sem.at[mine]
         for t in range(4):
             for dz in range(2):
                 dest_rz = rs[4 * dz] // 4 * 4
                 for d in range(8):
                     dest_q = qs[d]
                     dest_r = dest_rz + lax.rem(mine + 16 - t - dest_q // 4 * 2 - dest_q % 4, 4)
-                    src = send_right.at[u, dest_r, dest_q]
+                    src = send_right.at[dest_r, dest_q]
                     if dz or d:
                         push(src, slot, send_sem, recv_sem, (dest_r, cols[d]))
-                        continue
-                    here = dest_r == r
-
-                    @pl.when(here)
-                    def _():
-                        pltpu.make_async_copy(src, slot, recv_sem).start()
-
-                    @pl.when(jnp.logical_not(here))
-                    def _():
-                        push(src, slot, send_sem, recv_sem, (dest_r, cols[d]))
-
-    def give_halves(group, values):
-        for half in range(2):
-            for one in range(2):
-                low, high = (
-                    jnp.concatenate([v[one, at : at + 8] for v in values], axis=0).astype(BF16)
-                    for at in (8 * half, 8 * half + 16)
-                )
-                for m in range(4):
-                    lanes = slice(128 * m, 128 * m + 128)
-                    first, second = interleave(low[:, lanes], high[:, lanes])
-                    send_half[half, place_of(group, one), 2 * m] = first
-                    send_half[half, place_of(group, one), 2 * m + 1] = second
+                    else:
+                        push_or_keep(dest_r == r, src, slot, send_sem, recv_sem, (dest_r, cols[d]))
+
+    def give_half(half, members, values):
+        for one, dest_q in enumerate(members):
+            low, high = (
+                jnp.concatenate([v[one, at : at + 8] for v in values], axis=0).astype(BF16) for at in (0, 8)
+            )
+            for m in range(4):
+                lanes = slice(128 * m, 128 * m + 128)
+                first, second = interleave(low[:, lanes], high[:, lanes])
+                send_half[half, dest_q, 2 * m] = first
+                send_half[half, dest_q, 2 * m + 1] = second
 
     def give_whole(group, c, value):
         for one in range(2):
@@ -224,30 +259,21 @@
                 send_whole[place_of(group, one), 2 * m, c] = first
                 send_whole[place_of(group, one), 2 * m + 1, c] = second
 
-    def send_back(src, slot, send_sem, recv_sem, group):
-        for one in range(2):
-            dest_q = place_of(group, one)
+    def send_back(src, slot, send_sem, recv_sem, members):
+        for dest_q in members:
             dest_col = dest_q * 2 + core
-            here = dest_q == q
-
-            @pl.when(here)
-            def _():
-                pltpu.make_async_copy(src.at[dest_q, r], slot, recv_sem).start()
-
-            @pl.when(jnp.logical_not(here))
-            def _():
-                push(src.at[dest_q, r], slot, send_sem, recv_sem, (r, dest_col))
-
+            push_or_keep(dest_q == q, src.at[dest_q, r], slot, send_sem, recv_sem, (r, dest_col))
             for d in range(1, 8):
                 push(src.at[dest_q, rs[d]], slot, send_sem, recv_sem, (rs[d], dest_col))
 
-    def send_half_back(half, group):
+    def send_half_back(half, members):
         send_back(
-            send_half.at[half], recv_half.at[half, chip], mixed_send_sem.at[half], mixed_recv_sem.at[half], group
+            send_half.at[half], recv_half.at[half, chip], mixed_send_sem.at[half], mixed_recv_sem.at[half], members
         )
 
     def send_whole_back(group):
-        send_back(send_whole, recv_whole.at[chip], mixed_send_sem.at[2], mixed_recv_sem.at[2], group)
+        members = [place_of(group, one) for one in range(2)]
+        send_back(send_whole, recv_whole.at[chip], mixed_send_sem.at[2], mixed_recv_sem.at[2], members)
 
     def wait_all(ref, sem):
         pltpu.make_async_copy(ref, ref, sem).wait()
@@ -270,30 +296,37 @@
                 device_id_type=MESH,
             )
 
-        def finish_group(t):
-            group = turns[t]
+        def members_of(t):
+            return [2 * one + sets[t % 2] for one in range(4)]
+
+        def finish(t):
             half_copy(t).wait_recv()
             totals = [partial[t % 2, c, :, core] + half_recv[t, c].astype(F32) for c in range(2)]
-            give_halves(group, totals)
-            send_half_back(0, group)
+            give_half(t // 2, members_of(t), totals)
+            send_half_back(t // 2, members_of(t))
 
         for t in range(4):
-            group = turns[t]
-            wait_all(recv_right.at[0, group], right_recv_sem.at[0, group])
+            half, which = t // 2, sets[t % 2]
+            wait_all(recv_right0.at[half, which], right_recv0_sem.at[half, which])
+            for piece in range(4):
+                lanes = slice(32 * piece, 32 * piece + 32)
+                block = jnp.concatenate([recv_right0[half, which, one, :, :, lanes] for one in range(4)], axis=-1)
+                high, part = piece // 2, piece % 2
+                for c in range(2):
+                    right_op[c, part, :, 8 * high : 8 * high + 8] = block[:, 8 * c : 8 * c + 8]
             for c in range(2):
-                first, second = interleave(recv_right[0, group, 0, :, c], recv_right[0, group, 1, :, c])
-                right = jnp.concatenate([first.reshape(128, 128), second.reshape(128, 128)], axis=0)
                 product = lax.dot_general(
-                    right, left_op0[c].reshape(256, 512), (((0,), (0,)), ((), ())), preferred_element_type=F32
+                    right_op[c].reshape(256, 128),
+                    left_op0[c].reshape(256, 512),
+                    (((0,), (0,)), ((), ())),
+                    preferred_element_type=F32,
                 )
-                partial[t % 2, c] = product.reshape(2, 2, 32, 512)
+                partial[t % 2, c] = product.reshape(4, 2, 16, 512)
                 half_send[t, c] = partial[t % 2, c, :, 1 - core].astype(BF16)
             half_copy(t).start()
             if t:
-                finish_group(t - 1)
-        finish_group(3)
-        for t in range(4):
-            send_half_back(1, turns[t])
+                finish(t - 1)
+        finish(3)
         for t in range(4):
             half_copy(t).wait_send()
 
@@ -303,7 +336,7 @@
                 pieces = interleave(ref[half, :, 2 * m], ref[half, :, 2 * m + 1])
                 for part in range(2):
                     for c in range(2):
-                        left_op1[c, :, which, part, 8 * half : 8 * half + 8, 128 * m : 128 * m + 128] = pieces[
+                        left_op1[c, :, half, which, 8 * part : 8 * part + 8, 128 * m : 128 * m + 128] = pieces[
                             part
                         ][:, 8 * c : 8 * c + 8]
 
@@ -327,12 +360,12 @@
 
         for t in range(4):
             group = turns[t]
-            wait_all(recv_right.at[1, group], right_recv_sem.at[1, group])
+            wait_all(recv_right.at[group], right_recv_sem.at[group])
             for c in range(2):
                 columns = []
                 for m in range(4):
-                    even = recv_right[1, group, :, 2 * m, c]
-                    odd = recv_right[1, group, :, 2 * m + 1, c]
+                    even = recv_right[group, :, 2 * m, c]
+                    odd = recv_right[group, :, 2 * m + 1, c]
                     columns.append(jnp.stack(interleave(even, odd), axis=1).reshape(64, 128))
                 right = jnp.concatenate(columns, axis=1)
                 product = lax.dot_general(
@@ -366,33 +399,36 @@
             updated = state[t] + gating[t] * output
             for h in range(2):
                 block = updated[:, 128 * h : 128 * h + 128].T.astype(BF16)
-                final[:, 2 * t + h] = block.reshape(2, 64, 128)
+                final[:, 2 * t + h] = swap_blocks(block.reshape(2, 64, 128), 1)
             for part in range(2):
+                column = 16 * (t // 4) + 8 * part + 2 * t % 8
                 pltpu.make_async_copy(
-                    final.at[part, pl.ds(2 * t, 2)], out_ref.at[pl.ds(16 * part + 2 * t, 2)], out_sem
+                    final.at[part, pl.ds(2 * t, 2)], out_ref.at[pl.ds(column, 2)], out_sem
                 ).start()
 
     whole_left(0)
     pl.semaphore_wait(barrier, 64)
     send_whole_left()
-    whole_right(0)
-    send_all_right(0)
+    half_rights()
+    for half in range(2):
+        send_half_right(half)
     gate(0)
     outgoing()
     for half in range(2):
         absorb_half(half)
         half_left(half)
         send_half_left(half)
-    whole_right(1)
-    send_all_right(1)
+    whole_right()
+    send_whole_right()
     gate(1)
     incoming()
     absorb_whole()
 
     for half in range(2):
         wait_all(recv_half.at[half, pl.ds(0, 63)], left_send_sem.at[half])
+        wait_all(recv_half.at[half, pl.ds(0, 63)], right_send_sem.at[half])
         wait_all(recv_half.at[half, pl.ds(0, 63)], mixed_send_sem.at[half])
-    for sem in (left_send_sem.at[2], right_send_sem.at[0], right_send_sem.at[1], mixed_send_sem.at[2]):
+    for sem in (left_send_sem.at[2], right_send_sem.at[2], mixed_send_sem.at[2]):
         wait_all(recv_whole.at[pl.ds(0, 63)], sem)
     wait_all(out_ref, out_sem)
 
@@ -418,24 +454,28 @@
             pltpu.VMEM((2, 16, 64, 128), BF16),
             pltpu.VMEM((2, 2, 8, 16, 512), BF16),
             pltpu.VMEM((2, 8, 2, 2, 16, 512), BF16),
-            pltpu.VMEM((2, 2, 2, 2, 32, 512), F32),
+            pltpu.VMEM((2, 2, 4, 2, 16, 512), F32),
             pltpu.VMEM((8, 8, 2, 16, 128), BF16),
             pltpu.VMEM((2, 8, 8, 16, 128), BF16),
-            pltpu.VMEM((2, 8, 8, 2, 16, 128), BF16),
+            pltpu.VMEM((2, 8, 8, 16, 128), BF16),
+            pltpu.VMEM((8, 8, 2, 16, 128), BF16),
             pltpu.VMEM((8, 8, 2, 16, 128), BF16),
             pltpu.VMEM((2, 8, 8, 16, 128), BF16),
-            pltpu.VMEM((2, 4, 2, 8, 2, 16, 128), BF16),
+            pltpu.VMEM((2, 2, 4, 8, 16, 128), BF16),
+            pltpu.VMEM((4, 2, 8, 2, 16, 128), BF16),
+            pltpu.VMEM((2, 2, 8, 16, 128), BF16),
             pltpu.VMEM((2, 8, 8, 16, 128), BF16),
-            pltpu.VMEM((4, 2, 2, 32, 512), BF16),
-            pltpu.VMEM((4, 2, 2, 32, 512), BF16),
+            pltpu.VMEM((4, 2, 4, 16, 512), BF16),
+            pltpu.VMEM((4, 2, 4, 16, 512), BF16),
             pltpu.VMEM((2, 8, 8, 16, 128), BF16),
             pltpu.VMEM((2, 64, 16, 128), BF16),
             pltpu.VMEM((8, 8, 2, 16, 128), BF16),
             pltpu.VMEM((64, 2, 16, 128), BF16),
             dma((3,)),
             dma((3,)),
-            dma((2,)),
-            dma((2, 4)),
+            dma((3,)),
+            dma((2, 2)),
+            dma((4,)),
             dma((2,)),
             dma((2,)),
             dma((4,)),

time: 60.8 us -> 59.7 us (0.982)
  Pallas kernels: 58.5 us -> 57.4 us
    pallas_call x1, Pallas kernels: 58.5 us -> 57.4 us  [shards(): pl.pallas_call(kernel, out_shape=jax.ShapeDtypeStruct((32, 64, 128), BF16...]
where the time goes in v5:
time: 59.7 us; the launch traced here: 59.6 us
  Pallas kernels  57.4 us (96%)
  local copies, waits for them, and re-layouts  2.18 us (4%)
    pallas_call x1, Pallas kernels, shards(): pl.pallas_call(kernel, out_shape=jax.ShapeDtypeStruct((32, 64, 128), BF16...  57.4 us
    transpose x1, local copies, waits for them, and re-layouts, shards(): return jnp.transpose(out, (1, 0, 2))  2.18 us

profile of v5, /device:TPU:0, one launch (start us, length us, event | category | flops | bytes accessed | tf_op | source)
XLA Modules:
  0.0 59.6 jit_solution(9590624826423993952)
XLA Ops:
  0.0 57.4 %shard_map.37 = bf16[32,64,128]{2,1,0:T(8,128)(2,1)} custom-call(bf16[64,32,128]{2,1,0:T(8,128)(2,1)} %pair_hbm.1, bf16[2,128,640]{2,1,0:T(8,128)(2,1)} %proj_hbm.1, bf16[2,128,128]{2,1,0:T(8,128)(2,1)} %out_proj_hbm.1), custom_call_target="tpu_custom_call" | custom-call | tf_op jit(solution)/shard_map/pallas_call | solution.py:438
  57.4 2.2 %copy.4 = bf16[64,32,128]{2,1,0:T(8,128)(2,1)} copy(bf16[64,32,128]{2,0,1:T(8,128)(2,1)} %bitcast.1) | data formatting | bytes 1048576 | tf_op jit(solution)/shard_map/transpose | solution.py:492

commit v6 on v5

--- a/solution.py
+++ b/solution.py
@@ -105,7 +105,13 @@
     sets = [lax.rem(r + q + t, 2) for t in range(2)]
     cols = [dest_q * 2 + core for dest_q in qs]
     sibling = (r, q * 2 + 1 - core)
-    others = [(d // 8, d % 8) for d in sorted(range(1,64), key=lambda e: (e * 7919) % 1009)]
+    def hops(d, turn):
+        return d // 4 * turn + min(d % 4, 4 - d % 4)
+
+    far_r = sorted(range(8), key=lambda d: -hops(d, 2))
+    far_q = sorted(range(8), key=lambda d: -hops(d, 1))
+    others = [(d // 8, d % 8) for d in sorted(range(1, 64), key=lambda e: (e * 7919) % 1009)]
+    others.sort(key=lambda d: -hops(d[0], 2) - hops(d[1], 1))
 
     loads = [
         pltpu.make_async_copy(src, dst, load_sem.at[i])
@@ -214,12 +220,12 @@
         slot = recv_right0.at[half, mine, r // 2, q]
         send_sem, recv_sem = right_send_sem.at[half], right_recv0_sem.at[half, mine]
         for t in range(2):
-            for d in range(32):
-                dest_q = qs[d % 8]
-                dest_r = lax.rem(r // 2 + d // 8, 4) * 2 + lax.rem(mine + t + dest_q, 2)
-                col = cols[d % 8]
+            for a, d in [(a, d) for d in far_q for a in (2, 3, 1, 0)]:
+                dest_q = qs[d]
+                dest_r = lax.rem(r // 2 + a, 4) * 2 + lax.rem(mine + t + dest_q, 2)
+                col = cols[d]
                 src = send_right0.at[half, dest_r, dest_q]
-                if d:
+                if a or d:
                     push(src, slot, send_sem, recv_sem, (dest_r, col))
                 else:
                     push_or_keep(dest_r == r, src, slot, send_sem, recv_sem, (dest_r, col))
@@ -229,9 +235,9 @@
         slot = recv_right.at[mine, q % 4 // 2, r]
         send_sem, recv_sem = right_send_sem.at[2], right_recv_sem.at[mine]
         for t in range(4):
-            for dz in range(2):
+            for dz in (1, 0):
                 dest_rz = rs[4 * dz] // 4 * 4
-                for d in range(8):
+                for d in far_q:
                     dest_q = qs[d]
                     dest_r = dest_rz + lax.rem(mine + 16 - t - dest_q // 4 * 2 - dest_q % 4, 4)
                     src = send_right.at[dest_r, dest_q]
@@ -260,11 +266,13 @@
                 send_whole[place_of(group, one), 2 * m + 1, c] = second
 
     def send_back(src, slot, send_sem, recv_sem, members):
-        for dest_q in members:
-            dest_col = dest_q * 2 + core
-            push_or_keep(dest_q == q, src.at[dest_q, r], slot, send_sem, recv_sem, (r, dest_col))
-            for d in range(1, 8):
-                push(src.at[dest_q, rs[d]], slot, send_sem, recv_sem, (rs[d], dest_col))
+        for d in far_r:
+            for dest_q in members:
+                dest = (rs[d], dest_q * 2 + core)
+                if d:
+                    push(src.at[dest_q, rs[d]], slot, send_sem, recv_sem, dest)
+                else:
+                    push_or_keep(dest_q == q, src.at[dest_q, r], slot, send_sem, recv_sem, dest)
 
     def send_half_back(half, members):
         send_back(

time: 59.7 us -> 58.1 us (0.973)
  Pallas kernels: 57.4 us -> 55.8 us
    pallas_call x1, Pallas kernels: 57.4 us -> 55.8 us  [shards(): pl.pallas_call(kernel, out_shape=jax.ShapeDtypeStruct((32, 64, 128), BF16...]
where the time goes in v6:
time: 58.1 us; the launch traced here: 58 us
  Pallas kernels  55.8 us (96%)
  local copies, waits for them, and re-layouts  2.18 us (4%)
    pallas_call x1, Pallas kernels, shards(): pl.pallas_call(kernel, out_shape=jax.ShapeDtypeStruct((32, 64, 128), BF16...  55.8 us
    transpose x1, local copies, waits for them, and re-layouts, shards(): return jnp.transpose(out, (1, 0, 2))  2.18 us

profile of v6, /device:TPU:0, one launch (start us, length us, event | category | flops | bytes accessed | tf_op | source)
XLA Modules:
  0.0 58.0 jit_solution(5502962211029122332)
XLA Ops:
  0.0 55.8 %shard_map.37 = bf16[32,64,128]{2,1,0:T(8,128)(2,1)} custom-call(bf16[64,32,128]{2,1,0:T(8,128)(2,1)} %pair_hbm.1, bf16[2,128,640]{2,1,0:T(8,128)(2,1)} %proj_hbm.1, bf16[2,128,128]{2,1,0:T(8,128)(2,1)} %out_proj_hbm.1), custom_call_target="tpu_custom_call" | custom-call | tf_op jit(solution)/shard_map/pallas_call | solution.py:446
  55.8 2.2 %copy.4 = bf16[64,32,128]{2,1,0:T(8,128)(2,1)} copy(bf16[64,32,128]{2,0,1:T(8,128)(2,1)} %bitcast.1) | data formatting | bytes 1048576 | tf_op jit(solution)/shard_map/transpose | solution.py:500

commit v7 on v6

--- a/solution.py
+++ b/solution.py
@@ -311,7 +311,8 @@
             half_copy(t).wait_recv()
             totals = [partial[t % 2, c, :, core] + half_recv[t, c].astype(F32) for c in range(2)]
             give_half(t // 2, members_of(t), totals)
-            send_half_back(t // 2, members_of(t))
+            if t != 2:
+                send_half_back(t // 2, members_of(t) if t < 2 else members_of(2) + members_of(3))
 
         for t in range(4):
             half, which = t // 2, sets[t % 2]

time: 58.1 us -> 57.9 us (level)
  Pallas kernels: 55.8 us -> 55.2 us
where the time goes in v7:
time: 57.9 us; the launch traced here: 57.4 us
  Pallas kernels  55.2 us (95%)
  local copies, waits for them, and re-layouts  2.18 us (4%)
    pallas_call x1, Pallas kernels, shards(): pl.pallas_call(kernel, out_shape=jax.ShapeDtypeStruct((32, 64, 128), BF16...  55.2 us
    transpose x1, local copies, waits for them, and re-layouts, shards(): return jnp.transpose(out, (1, 0, 2))  2.18 us

profile of v7, /device:TPU:0, one launch (start us, length us, event | category | flops | bytes accessed | tf_op | source)
XLA Modules:
  0.0 57.4 jit_solution(263087002342583135)
XLA Ops:
  0.0 55.2 %shard_map.37 = bf16[32,64,128]{2,1,0:T(8,128)(2,1)} custom-call(bf16[64,32,128]{2,1,0:T(8,128)(2,1)} %pair_hbm.1, bf16[2,128,640]{2,1,0:T(8,128)(2,1)} %proj_hbm.1, bf16[2,128,128]{2,1,0:T(8,128)(2,1)} %out_proj_hbm.1), custom_call_target="tpu_custom_call" | custom-call | tf_op jit(solution)/shard_map/pallas_call | solution.py:447
  55.2 2.2 %copy.4 = bf16[64,32,128]{2,1,0:T(8,128)(2,1)} copy(bf16[64,32,128]{2,0,1:T(8,128)(2,1)} %bitcast.1) | data formatting | bytes 1048576 | tf_op jit(solution)/shard_map/transpose | solution.py:501
